TPU v7x, 512 devices: a whole 4x8x8 slice. The times are simulated.
512 devices in a mesh: section: 16 (over y, core), ctx: 8 (over z), tp: 4 (over x).
Axes of the slice: x: 4, y: 8, z: 8, core: 2. Of those that a mesh axis runs over, the one named last changes fastest.
Arguments:
- query_rows: bfloat16 [16, 1024, 16384], P('section', 'ctx', 'tp'), may hold values from -56 to 56
- key_rows: bfloat16 [16, 1024, 1024], P('section', 'ctx', 'tp'), may hold values from -16 to 16
- value_rows: bfloat16 [16, 1024, 1024], P('section', 'ctx', 'tp'), may hold values from -6 to 6
- positions: int32 [16, 1024], P('section'), may hold values from 0 to 131071, as said below
Outputs:
- attended: bfloat16 [16, 1024, 16384], P('section', 'ctx', 'tp')
Inputs may be any that keep to these rules, and one draw needn't show every extreme that they name: For each section, the 1024 positions are the run start, start + 1, ..., start + 1023 laid out in blocks of 64 consecutive ascending positions whose order along the sequence dimension is a permutation of the 16 blocks; start is 0 for section 0 and 130048 for section 15.
All inputs are finite; a program needn't handle non-finite values.
Results may differ from a plain program's by a relative error of at most 0.0084.
Values may be sent and summed in bfloat16 or wider, within the bound.
No kernel may reach another device: no remote copies, remote signals or barrier semaphores. Data moves between devices by JAX's collectives and lax.ppermute only.
A program may use at most 64 MiB of HBM per device.

v0:
```python
from functools import partial
import math

import jax
import jax.numpy as jnp
import numpy as np
from jax import lax
from jax.sharding import PartitionSpec as P

HEAD_DIM = 128


def shifted(block, axis, distance):
    devices = range(lax.axis_size(axis))
    route = [((i - distance) % len(devices), i) for i in devices]
    return lax.ppermute(block, axis, route)


def rope_tables(head_size):
    index_ids = np.arange(head_size // 2) * 1.0
    natural = 500000.0 ** (-2.0 * index_ids / head_size)
    wavelength = 2.0 * math.pi / natural
    smooth = (8192.0 / wavelength - 1.0) / 3.0
    blended = (1.0 - smooth) * natural / 8.0 + smooth * natural
    scaled = np.where(
        wavelength < 2048.0, natural, np.where(wavelength > 8192.0, natural / 8.0, blended)
    )
    coarse = np.mod(1024.0 * scaled, 2.0 * math.pi)
    return (jnp.asarray(scaled, jnp.float32), jnp.asarray(coarse, jnp.float32))


def rotate(row_data, token_pos, head_count):
    count_rows = row_data.shape[0]
    head_size = row_data.shape[1] // head_count
    fine_freq, coarse = rope_tables(head_size)
    upper_part = (token_pos // 1024).astype(jnp.float32)
    lower_part = (token_pos % 1024).astype(jnp.float32)
    angles = upper_part[:, None] * coarse[None, :] + lower_part[:, None] * fine_freq[None, :]
    cosine = jnp.cos(angles)[:, None, :]
    sine_part = jnp.sin(angles)[:, None, :]
    heads_data = row_data.reshape(count_rows, head_count, head_size).astype(jnp.float32)
    front_half = heads_data[..., : head_size // 2]
    back_half = heads_data[..., head_size // 2 :]
    turned = jnp.concatenate(
        [front_half * cosine - back_half * sine_part, back_half * cosine + front_half * sine_part],
        axis=-1,
    )
    return turned.reshape(count_rows, head_count * head_size).astype(jnp.bfloat16)


def attend_block(state_now, queries, key_block, value_block, query_pos, key_pos):
    running_max, denominator, numerator = state_now
    scores = jnp.einsum(
        "tkgd,skd->tkgs", queries, key_block, preferred_element_type=jnp.float32
    ) / math.sqrt(queries.shape[-1])
    allowed = key_pos[None, None, None, :] <= query_pos[:, None, None, None]
    masked = jnp.where(allowed, scores, -1e30)
    new_max = jnp.maximum(running_max, jnp.max(masked, axis=-1))
    exponent = jnp.where(allowed, jnp.exp(masked - new_max[..., None]), 0.0)
    factor = jnp.exp(running_max - new_max)
    denominator = denominator * factor + jnp.sum(exponent, axis=-1)
    weights = exponent.astype(jnp.bfloat16)
    numerator = numerator * factor[..., None] + jnp.einsum(
        "tkgs,skd->tkgd", weights, value_block, preferred_element_type=jnp.float32
    )
    return (new_max, denominator, numerator)


def fold_keys(queries, query_pos, latest, position_table, key_heads, state_now, pieces, offset):
    key_piece, value_piece = pieces
    piece_rows = key_piece.shape[0]
    for lower_row in range(0, piece_rows, 512):
        block_size = min(512, piece_rows - lower_row)
        key_block = key_piece[lower_row : lower_row + block_size].reshape(
            block_size, key_heads, HEAD_DIM
        )
        value_block = value_piece[lower_row : lower_row + block_size].reshape(
            block_size, key_heads, HEAD_DIM
        )
        key_pos = lax.dynamic_slice_in_dim(position_table, lower_row, block_size)
        state_now = attend_block(state_now, queries, key_block, value_block, query_pos, key_pos)
    return state_now


def per_device(query_rows, key_rows, value_rows, positions):
    local_rows = query_rows.shape[1]
    key_heads = key_rows.shape[2] // HEAD_DIM
    query_heads = query_rows.shape[2] // HEAD_DIM
    groups = query_heads // key_heads
    owner_index = lax.axis_index("ctx")
    initial = (
        jnp.full((local_rows, key_heads, groups), -1e30, jnp.float32),
        jnp.zeros((local_rows, key_heads, groups), jnp.float32),
        jnp.zeros((local_rows, key_heads, groups, HEAD_DIM), jnp.float32),
    )
    position_table = positions[0]
    own_pos = lax.dynamic_slice_in_dim(position_table, owner_index * local_rows, local_rows)
    latest = jnp.max(own_pos)
    query_in, key_in, value_in = shifted((query_rows, key_rows, value_rows), "section", 1)
    rotated_keys = rotate(key_in[0], own_pos, key_heads)
    rotated_queries = rotate(query_in[0], own_pos, query_heads).reshape(
        local_rows, key_heads, groups, HEAD_DIM
    )
    folding = partial(fold_keys, rotated_queries, own_pos, latest, position_table, key_heads)
    final_state = folding(
        initial,
        (
            lax.all_gather(rotated_keys, "ctx", axis=0, tiled=True),
            lax.all_gather(value_in[0], "ctx", axis=0, tiled=True),
        ),
        jnp.int32(0),
    )
    running_max, denominator, numerator = final_state
    result = (numerator / denominator[..., None]).astype(jnp.bfloat16)
    return result.reshape(1, local_rows, query_heads * HEAD_DIM)


def solution(mesh):
    return jax.shard_map(
        per_device,
        mesh=mesh,
        in_specs=(
            P("section", "ctx", "tp"),
            P("section", "ctx", "tp"),
            P("section", "ctx", "tp"),
            P("section", None),
        ),
        out_specs=P("section", "ctx", "tp"),
        check_vma=False,
    )
```

profile of v0, /device:TPU:6, one launch (start us, length us, event | category | flops | bytes accessed | tf_op | source)
XLA Modules:
  0.0 90.9 jit_solution(3598295213996838895)
XLA Ops:
  0.0 0.0 collective-permute-start.1
  0.0 1.7 %collective-permute-start = (bf16[1,128,256]{2,1,0:T(8,128)(2,1)}, bf16[1,128,256]{2,1,0:T(8,128)(2,1)S(1)}, u32[]{:S(2)}, u32[]{:S(2)}) collective-permute-start(bf16[1,128,256]{2,1,0:T(8,128)(2,1)} %param.9), channel_id=1, source_target_pairs={{480,0},{0,32},{32,64},{64,96},{96,128},{128,160},{160,192},{192,2... | collective-permute-start | bytes 196616 | tf_op jit(solution)/shard_map/ppermute | solution.py:16
  1.7 0.0 collective-permute-start.2
  1.7 0.7 fusion.31
  2.4 0.7 fusion.20
  3.1 0.2 broadcast_compare_fusion
  3.3 0.9 fusion.18
  4.2 0.1 copy.32
  4.3 0.1 copy.34
  4.4 12.7 %collective-permute-done.2 = bf16[1,128,256]{2,1,0:T(8,128)(2,1)S(1)} collective-permute-done((bf16[1,128,256]{2,1,0:T(8,128)(2,1)}, bf16[1,128,256]{2,1,0:T(8,128)(2,1)S(1)}, u32[]{:S(2)}, u32[]{:S(2)}) %collective-permute-start.2) | collective-permute-done | bytes 65568 | tf_op jit(solution)/shard_map/ppermute | solution.py:16
  17.1 32.0 %all-gather = bf16[1,1024,256]{2,1,0:T(8,128)(2,1)S(1)} all-gather(bf16[1,128,256]{2,1,0:T(8,128)(2,1)S(1)} %collective-permute-done.2), channel_id=2, replica_groups=mesh['section'=16,'ctx'=8,'tp'=4] {'ctx'}, dimensions={1}, use_global_device_ids=true | all-gather | bytes 589824 | tf_op jit(solution)/shard_map/all_gather | solution.py:109
  49.1 0.1 copy.36
  49.3 0.1 copy.39
  49.4 0.0 collective-permute-done
  49.4 0.1 copy.52
  49.6 23.1 %all_gather.6 = bf16[1024,256]{0,1:T(8,128)(2,1)S(1)} all-gather(bf16[128,256]{0,1:T(8,128)(2,1)S(1)} %bitcast.82), channel_id=1, replica_groups=mesh['section'=16,'ctx'=8,'tp'=4] {'ctx'}, dimensions={0}, use_global_device_ids=true | all-gather | bytes 589824 | tf_op jit(solution)/shard_map/all_gather | solution.py:108
  72.7 0.0 collective-permute-done.1
  72.8 0.2 convert_bitcast_fusion
  73.0 0.4 copy.55
  73.3 0.7 fusion.28
  74.1 2.4 %subtract_convert_fusion = (bf16[128,32,64]{2,0,1:T(8,128)(2,1)S(1)}, bf16[128,32,64]{2,0,1:T(8,128)(2,1)S(1)}) fusion(f32[128,32,64]{2,1,0:T(8,128)S(1)} %get-tuple-element.12, f32[128,32,64]{2,1,0:T(8,128)S(1)} %get-tuple-element.11, f32[128,64]{1,0:T(8,128)S(1)} %copy.34, f32[128,64]{1,0:T(8,128)S(1)} %copy.32), kind=kLoop, calls=%fused_computation.21 | loop fusion | flops 2097152 | bytes 3211264 | tf_op jit(solution)/shard_map/convert.2
  76.5 0.6 pad_maximum_fusion
  77.1 1.4 %fusion.1 = (f32[128,2,16]{0,2,1:T(8,128)S(1)}, f32[2,512,128,16]{2,1,3,0:T(8,128)S(1)}) fusion(pred[128,512]{0,1:T(8,128)(4,1)S(1)} %get-tuple-element.26, bf16[512,2,128,1]{0,2,3,1:T(8,128)(2,1)S(1)} %bitcast.80, bf16[128,2,16,128]{3,0,2,1:T(8,128)(2,1)S(1)} %bitcast.76), kind=kOutput, calls=%fused_computation.5 | convolution fusion | flops 543158272 | bytes 9781248 | tf_op jit(solution)/shard_map/tkgd,skd->tkgs/dot_general | solution.py:53
  78.6 1.4 %fusion = (f32[128,2,16]{0,2,1:T(8,128)S(1)}, f32[2,512,128,16]{2,1,3,0:T(8,128)S(1)}) fusion(pred[128,512]{0,1:T(8,128)(4,1)S(1)} %get-tuple-element.27, bf16[512,2,128,1]{0,2,3,1:T(8,128)(2,1)S(1)} %bitcast.79, bf16[128,2,16,128]{3,0,2,1:T(8,128)(2,1)S(1)} %bitcast.77), kind=kOutput, calls=%fused_computation.4 | convolution fusion | flops 543158272 | bytes 9781248 | tf_op jit(solution)/shard_map/tkgd,skd->tkgs/dot_general | solution.py:53
  80.0 2.2 %fusion.8 = f32[2,128,16,128]{1,3,2,0:T(8,128)S(1)} fusion(bf16[512,2,128,1]{0,2,3,1:T(8,128)(2,1)S(1)} %bitcast.84, f32[2,512,128,16]{2,1,3,0:T(8,128)S(1)} %get-tuple-element.29, f32[128,2,16]{0,2,1:T(8,128)S(1)} %get-tuple-element.21, pred[128,512]{0,1:T(8,128)(4,1)S(1)} %get-tuple-element.27), kind=kOutput, calls=%fused_computation.11 | convolution fusion | flops 547356672 | bytes 10829824 | tf_op jit(solution)/shard_map/tkgs,skd->tkgd/dot_general | solution.py:63
  82.2 4.8 %fusion.2 = (f32[128,2,16]{0,2,1:T(8,128)S(1)}, f32[128,2,16]{0,2,1:T(8,128)S(1)}) fusion(f32[2,512,128,16]{2,1,3,0:T(8,128)S(1)} %get-tuple-element.29, f32[128,2,16]{0,2,1:T(8,128)S(1)} %get-tuple-element.21, pred[128,512]{0,1:T(8,128)(4,1)S(1)} %get-tuple-element.27, f32[128,2,16]{0,2,1:T(8,128)S(1)} %get-tuple-element.20, ...), kind=kLoop, calls=%fused_computation.6 | loop fusion | flops 20963328 | bytes 16973824 | tf_op jit(solution)/shard_map/reduce_sum | solution.py:61
  87.0 2.6 %fusion.13 = bf16[128,2,16,128]{0,3,2,1:T(8,128)(2,1)S(1)} fusion(f32[2,128,16,128]{1,3,2,0:T(8,128)S(1)} %fusion.8, bf16[512,2,128,1]{0,2,3,1:T(8,128)(2,1)S(1)} %bitcast.83, f32[2,512,128,16]{2,1,3,0:T(8,128)S(1)} %get-tuple-element.31, f32[128,2,16]{0,2,1:T(8,128)S(1)} %get-tuple-element.20, pred[128,512]{0,1:T(8,128)(4,1)S(1)} %get-tuple-element.26, ...), kind=kOutput, calls=%fused_computation.16 | convolution fusion | flops 549978112 | bytes 11927552 | tf_op jit(solution)/shard_map/tkgs,skd->tkgd/dot_general | solution.py:63
  89.6 1.3 %copy.41 = bf16[1,128,4096]{2,1,0:T(8,128)(2,1)} copy(bf16[1,128,4096]{1,2,0:T(8,128)(2,1)S(1)} %bitcast.78) | data formatting | bytes 2097152 | tf_op jit(solution)/shard_map/reshape | solution.py:115
  (7 shorter events, 0.1 us)
Async XLA Ops:
  0.0 72.7 %collective-permute-start.1 = (bf16[1,128,4096]{2,1,0:T(8,128)(2,1)}, bf16[1,128,4096]{2,1,0:T(8,128)(2,1)S(1)}, u32[]{:S(2)}, u32[]{:S(2)}) collective-permute-start(bf16[1,128,4096]{2,1,0:T(8,128)(2,1)} %param.8), channel_id=1, source_target_pairs={{480,0},{0,32},{32,64},{64,96},{96,128},{128,160},{160,192},{192,2... | collective-permute-start | bytes 3145736 | tf_op jit(solution)/shard_map/ppermute | solution.py:16
  0.0 49.4 %collective-permute-start = (bf16[1,128,256]{2,1,0:T(8,128)(2,1)}, bf16[1,128,256]{2,1,0:T(8,128)(2,1)S(1)}, u32[]{:S(2)}, u32[]{:S(2)}) collective-permute-start(bf16[1,128,256]{2,1,0:T(8,128)(2,1)} %param.9), channel_id=1, source_target_pairs={{480,0},{0,32},{32,64},{64,96},{96,128},{128,160},{160,192},{192,2... | collective-permute-start | bytes 196616 | tf_op jit(solution)/shard_map/ppermute | solution.py:16
  1.7 15.4 %collective-permute-start.2 = (bf16[1,128,256]{2,1,0:T(8,128)(2,1)}, bf16[1,128,256]{2,1,0:T(8,128)(2,1)S(1)}, u32[]{:S(2)}, u32[]{:S(2)}) collective-permute-start(bf16[1,128,256]{2,1,0:T(8,128)(2,1)} %param.10), channel_id=1, source_target_pairs={{480,0},{0,32},{32,64},{64,96},{96,128},{128,160},{160,192},{192,2... | collective-permute-start | bytes 196616 | tf_op jit(solution)/shard_map/ppermute | solution.py:16
where the time goes:
time: 91.1 us; the launch traced here: 90.9 us
  blocking collectives  55.2 us (61%)
  waiting for transfers between devices  12.7 us (14%)
  other arithmetic  9.84 us (11%)
  matrix products  7.63 us (8%)
  local copies, waits for them, and re-layouts  3.74 us (4%)
  starting transfers between devices  1.72 us (2%)
    all_gather x1, blocking collectives, per_device(): lax.all_gather(value_in[0], 'ctx', axis=0, tiled=True)  32 us
    all_gather x1, blocking collectives, per_device(): lax.all_gather(rotated_keys, 'ctx', axis=0, tiled=True)  23.1 us
    ppermute x3, waiting for transfers between devices, shifted(): return lax.ppermute(block, axis, route)  12.7 us
    reduce_sum x1, other arithmetic, attend_block(): denominator = denominator * factor + jnp.sum(exponent, axis=-1)  4.79 us
    dot_general x2, matrix products, attend_block(): jnp.einsum('tkgs,skd->tkgd', weights, value_block, preferred_element_type...  4.77 us
    dot_general x2, matrix products, attend_block(): jnp.einsum('tkgd,skd->tkgs', queries, key_block, preferred_element_type=j...  2.86 us
    another operation x2, other arithmetic  2.47 us
  transfers between devices with their start and end apart: 3, of which 1 were waited for; matrix products, arithmetic and copies ran while one was open for 3% of the time, Pallas kernels for 0%

commit v1 on v0

v1 whole, which is shorter than its diff:
```python
from functools import partial
import math

import jax
import jax.numpy as jnp
import numpy as np
from jax import lax
from jax.experimental import pallas as pl
from jax.experimental.pallas import tpu as pltpu
from jax.sharding import PartitionSpec as P

HEAD_DIM = 128
MASKED = -1e30
SCALE = math.log2(math.e) / math.sqrt(HEAD_DIM)
HEADS_PER_PASS = 2


def shifted(block, axis, distance):
    devices = range(lax.axis_size(axis))
    route = [((i - distance) % len(devices), i) for i in devices]
    return lax.ppermute(block, axis, route)


def rope_tables(head_size):
    index_ids = np.arange(head_size // 2) * 1.0
    natural = 500000.0 ** (-2.0 * index_ids / head_size)
    wavelength = 2.0 * math.pi / natural
    smooth = (8192.0 / wavelength - 1.0) / 3.0
    blended = (1.0 - smooth) * natural / 8.0 + smooth * natural
    scaled = np.where(
        wavelength < 2048.0, natural, np.where(wavelength > 8192.0, natural / 8.0, blended)
    )
    coarse = np.mod(1024.0 * scaled, 2.0 * math.pi)
    return (jnp.asarray(scaled, jnp.float32), jnp.asarray(coarse, jnp.float32))


def turn_tables(token_pos):
    fine_freq, coarse = rope_tables(HEAD_DIM)
    upper_part = (token_pos // 1024).astype(jnp.float32)
    lower_part = (token_pos % 1024).astype(jnp.float32)
    angles = upper_part[:, None] * coarse[None, :] + lower_part[:, None] * fine_freq[None, :]
    cosine, sine = jnp.cos(angles), jnp.sin(angles)
    return (
        jnp.concatenate([cosine, cosine], axis=-1),
        jnp.concatenate([-sine, sine], axis=-1),
    )


def turned(head, cosine, sine):
    head = head.astype(jnp.float32)
    return (head * cosine + pltpu.roll(head, HEAD_DIM // 2, 1) * sine).astype(jnp.bfloat16)


def spread_kernel(key_ref, value_ref, cosine_ref, sine_ref, *outs):
    cosine, sine = cosine_ref[...], sine_ref[...]
    for head, out in enumerate(outs):
        columns = pl.ds(head * HEAD_DIM, HEAD_DIM)
        keys = turned(key_ref[:, columns], cosine, sine)
        values = value_ref[:, columns]
        for owner in range(out.shape[0]):
            out[owner, :, :HEAD_DIM] = keys
            out[owner, :, HEAD_DIM:] = values


def spread(key_in, value_in, cosine, sine, owners):
    rows = key_in.shape[0]
    key_heads = key_in.shape[1] // HEAD_DIM
    shape = jax.ShapeDtypeStruct((owners, rows, 2 * HEAD_DIM), jnp.bfloat16)
    return pl.pallas_call(
        spread_kernel,
        out_shape=[shape] * key_heads,
        name="spread",
    )(key_in, value_in, cosine, sine)


def turn_kernel(query_ref, cosine_ref, sine_ref, out_ref):
    cosine, sine = cosine_ref[...], sine_ref[...]
    rows = query_ref.shape[0]
    for head in range(query_ref.shape[1] // HEAD_DIM):
        out_ref[head * rows : (head + 1) * rows, :] = turned(
            query_ref[:, head * HEAD_DIM : (head + 1) * HEAD_DIM], cosine, sine
        )


def turn_queries(query_in, cosine, sine):
    rows, width = query_in.shape
    heads = width // HEAD_DIM
    steps = 4
    return pl.pallas_call(
        turn_kernel,
        grid=(steps,),
        in_specs=[
            pl.BlockSpec((rows, width // steps), lambda i: (0, i)),
            pl.BlockSpec((rows, HEAD_DIM), lambda i: (0, 0)),
            pl.BlockSpec((rows, HEAD_DIM), lambda i: (0, 0)),
        ],
        out_specs=pl.BlockSpec((heads // steps * rows, HEAD_DIM), lambda i: (i, 0)),
        out_shape=jax.ShapeDtypeStruct((heads * rows, HEAD_DIM), jnp.bfloat16),
        name="turn",
    )(query_in, cosine, sine)


def attend_kernel(query_ref, gathered_ref, mask_ref, *rest):
    out_ref = rest[-1]
    rows = mask_ref.shape[1]
    tokens = mask_ref.shape[0]
    gathered = gathered_ref[...].reshape(tokens, 2 * HEAD_DIM)
    keys = jnp.concatenate([gathered[:, :HEAD_DIM], mask_ref[...]], axis=1)
    values = jnp.concatenate(
        [gathered[:, HEAD_DIM:], jnp.ones((tokens, HEAD_DIM), jnp.bfloat16)], axis=1
    )
    size = HEADS_PER_PASS * rows
    own = lax.broadcasted_iota(jnp.int32, (size, rows), 0) % rows
    one_hot = (own == lax.broadcasted_iota(jnp.int32, (size, rows), 1)).astype(jnp.bfloat16)

    def score(step):
        queries = jnp.concatenate([query_ref[step * size : (step + 1) * size, :], one_hot], axis=1)
        return lax.dot_general(
            queries, keys, (((1,), (1,)), ((), ())), preferred_element_type=jnp.float32
        )

    steps = query_ref.shape[0] // size
    following = score(0)
    for step in range(steps):
        scores = following
        if step + 1 < steps:
            following = score(step + 1)
        highest = jnp.max(scores, axis=-1, keepdims=True)
        weights = jnp.exp2((scores - highest) * SCALE).astype(jnp.bfloat16)
        summed = lax.dot_general(
            weights, values, (((1,), (0,)), ((), ())), preferred_element_type=jnp.float32
        )
        attended = (summed[:, :HEAD_DIM] / summed[:, HEAD_DIM:]).astype(jnp.bfloat16)
        for i in range(HEADS_PER_PASS):
            head = step * HEADS_PER_PASS + i
            out_ref[:, head * HEAD_DIM : (head + 1) * HEAD_DIM] = attended[
                i * rows : (i + 1) * rows
            ]


def attend(queries, gathered, mask, so_far, group, group_count):
    tokens, rows = mask.shape
    per_group = queries.shape[0] // group_count
    width = per_group // rows * HEAD_DIM
    in_specs = [
        pl.BlockSpec((per_group, HEAD_DIM), lambda i: (group, 0)),
        pl.BlockSpec(gathered.shape, lambda i: (0, 0, 0)),
        pl.BlockSpec(mask.shape, lambda i: (0, 0)),
    ]
    operands = [queries, gathered, mask]
    aliases = {}
    if so_far is not None:
        in_specs.append(pl.BlockSpec(memory_space=pl.ANY))
        operands.append(so_far)
        aliases = {3: 0}
    products = 4 * per_group * tokens * 2 * HEAD_DIM
    return pl.pallas_call(
        attend_kernel,
        grid=(1,),
        in_specs=in_specs,
        out_specs=pl.BlockSpec((rows, width), lambda i: (0, group)),
        out_shape=jax.ShapeDtypeStruct((rows, width * group_count), jnp.bfloat16),
        input_output_aliases=aliases,
        compiler_params=pltpu.CompilerParams(vmem_limit_bytes=40 * 1024 * 1024),
        cost_estimate=pl.CostEstimate(
            flops=products, bytes_accessed=2 * per_group * HEAD_DIM * 2, transcendentals=per_group * tokens
        ),
        name="attend",
    )(*operands)


def per_device(query_rows, key_rows, value_rows, positions):
    local_rows = query_rows.shape[1]
    key_heads = key_rows.shape[2] // HEAD_DIM
    owners = lax.axis_size("ctx")
    key_in, value_in = shifted((key_rows, value_rows), "section", 1)
    position_table = positions[0]
    own_pos = lax.dynamic_slice_in_dim(
        position_table, lax.axis_index("ctx") * local_rows, local_rows
    )
    cosine, sine = turn_tables(own_pos)
    mask = jnp.where(position_table[:, None] <= own_pos[None, :], 0.0, MASKED).astype(jnp.bfloat16)
    query_rows, cosine, sine = lax.optimization_barrier((query_rows, cosine, sine))
    query_in = shifted(query_rows, "section", 1)
    pieces = spread(key_in[0], value_in[0], cosine, sine, owners)
    gathered = [lax.all_to_all(piece, "ctx", 0, 0, tiled=False) for piece in pieces]
    queries = turn_queries(query_in[0], cosine, sine)
    result = None
    for group in range(key_heads):
        result = attend(queries, gathered[group], mask, result, group, key_heads)
    return result[None]


def solution(mesh):
    return jax.shard_map(
        per_device,
        mesh=mesh,
        in_specs=(
            P("section", "ctx", "tp"),
            P("section", "ctx", "tp"),
            P("section", "ctx", "tp"),
            P("section", None),
        ),
        out_specs=P("section", "ctx", "tp"),
        check_vma=False,
    )
```

time: 91.1 us -> 61.7 us (0.68)
  the two profiles are of different devices: /device:TPU:6 before, /device:TPU:27 now
where the time goes in v1:
time: 61.7 us; the launch traced here: 61.2 us
  waiting for transfers between devices  22.7 us (37%)
  starting transfers between devices  20.3 us (33%)
  Pallas kernels  12.7 us (21%)
  local copies, waits for them, and re-layouts  4.17 us (7%)
  other arithmetic  1.3 us (2%)
    all_to_all x2, waiting for transfers between devices, per_device(): lax.all_to_all(piece, 'ctx', 0, 0, tiled=False)  22.7 us
    all_to_all x2, starting transfers between devices, per_device(): lax.all_to_all(piece, 'ctx', 0, 0, tiled=False)  13.6 us
    pallas_call x2, Pallas kernels, attend(): pl.pallas_call(attend_kernel, grid=(1,), in_specs=in_specs, out_specs=pl....  7.07 us
    ppermute x3, starting transfers between devices, shifted(): return lax.ppermute(block, axis, route)  6.66 us
    unnamed x18, local copies, waits for them, and re-layouts  4.17 us
    pallas_call x1, Pallas kernels, turn_queries(): pl.pallas_call(turn_kernel, grid=(steps,), in_specs=[pl.BlockSpec((rows,...  3.63 us
    pallas_call x1, Pallas kernels, spread(): pl.pallas_call(spread_kernel, out_shape=[shape] * key_heads, name='spread')  2.03 us
  transfers between devices with their start and end apart: 5, of which 2 were waited for; matrix products, arithmetic and copies ran while one was open for 2% of the time, Pallas kernels for 12%

profile of v1, /device:TPU:27, one launch (start us, length us, event | category | flops | bytes accessed | tf_op | source)
XLA Modules:
  0.0 61.2 jit_solution(16813000537305451279)
XLA Ops:
  0.0 3.1 %collective-permute-start.1 = (bf16[1,128,256]{2,1,0:T(8,128)(2,1)}, bf16[1,128,256]{2,1,0:T(8,128)(2,1)S(1)}, u32[]{:S(2)}, u32[]{:S(2)}) collective-permute-start(bf16[1,128,256]{2,1,0:T(8,128)(2,1)} %param.7), channel_id=1, source_target_pairs={{480,0},{0,32},{32,64},{64,96},{96,128},{128,160},{160,192},{192,2... | collective-permute-start | bytes 196616 | tf_op jit(solution)/shard_map/ppermute | solution.py:21
  3.1 0.0 collective-permute-start.2
  3.1 0.0 copy-start.5
  3.1 0.7 %copy-done.5 = s32[1,1024]{1,0:T(1,128)S(1)} copy-done((s32[1,1024]{1,0:T(1,128)S(1)}, s32[1,1024]{1,0:T(1,128)}, u32[]{:S(2)}) %copy-start.5) | copy-done | bytes 4120
  3.8 0.0 copy-start.6
  3.8 0.0 copy-start.7
  3.8 0.0 copy-start.8
  3.9 0.6 %copy-done.6 = f32[64]{0:T(128)S(1)} copy-done((f32[64]{0:T(128)S(1)}, f32[64]{0:T(128)}, u32[]{:S(2)}) %copy-start.6) | copy-done | bytes 280
  4.5 0.0 copy-done.7
  4.5 0.3 fusion.2
  4.8 0.8 %pad_maximum_fusion = (f32[128,128]{1,0:T(8,128)}, f32[128,128]{1,0:T(8,128)}) fusion(f32[128,64]{1,0:T(8,128)S(1)} %get-tuple-element.19, f32[128,64]{1,0:T(8,128)S(1)} %get-tuple-element.18, f32[128,64]{1,0:T(8,128)S(1)} %get-tuple-element.17), kind=kLoop, calls=%fused_computation.1 | loop fusion | flops 32768 | bytes 229376 | tf_op jit(solution)/shard_map/concatenate | solution.py:44
  5.6 0.0 collective-permute-done.1
  5.6 0.0 copy-start.3
  5.6 0.0 collective-permute-done.2
  5.6 0.0 copy-start.4
  5.6 0.6 copy-done.3
  6.2 0.0 copy-done.4
  6.2 2.0 %spread.1 = (bf16[8,128,256]{2,1,0:T(8,128)(2,1)}, bf16[8,128,256]{2,1,0:T(8,128)(2,1)}) custom-call(bf16[128,256]{1,0:T(8,128)(2,1)} %bitcast.9, bf16[128,256]{1,0:T(8,128)(2,1)} %bitcast.10, f32[128,128]{1,0:T(8,128)} %get-tuple-element.11.cosine_ref, f32[128,128]{1,0:T(8,128)} %get-tuple-element.12.sine_ref), custom_call_target="tpu_custom_call" | custom-call | tf_op jit(solution)/shard_map/spread/pallas_call | solution.py:69
  8.3 10.1 %all-to-all-start.1 = ((bf16[8,128,256]{2,1,0:T(8,128)(2,1)}), bf16[8,128,256]{2,1,0:T(8,128)(2,1)S(1)}, u32[]{:S(2)}, u32[]{:S(2)}) async-start(bf16[8,128,256]{2,1,0:T(8,128)(2,1)} %get-tuple-element.14), calls=%async_computation.1 | async-start | bytes 1048576 | tf_op jit(solution)/shard_map/all_to_all | solution.py:186
  18.4 0.0 copy-done.8
  18.4 3.6 %collective-permute-start = (bf16[1,128,4096]{2,1,0:T(8,128)(2,1)S(1)}, bf16[1,128,4096]{2,1,0:T(8,128)(2,1)S(1)}, u32[]{:S(2)}, u32[]{:S(2)}) collective-permute-start(bf16[1,128,4096]{2,1,0:T(8,128)(2,1)S(1)} %copy-done.8), channel_id=1, source_target_pairs={{480,0},{0,32},{32,64},{64,96},{96,128},{128,160},{160,192},{192,2... | collective-permute-start | bytes 3145736 | tf_op jit(solution)/shard_map/ppermute | solution.py:21
  21.9 14.4 %all-to-all-done.1.gathered_ref = bf16[8,128,256]{2,1,0:T(8,128)(2,1)S(1)} async-done(((bf16[8,128,256]{2,1,0:T(8,128)(2,1)}), bf16[8,128,256]{2,1,0:T(8,128)(2,1)S(1)}, u32[]{:S(2)}, u32[]{:S(2)}) %all-to-all-start.1) | async-done | bytes 524320 | tf_op jit(solution)/shard_map/all_to_all | solution.py:186
  36.3 3.5 %all-to-all-start = ((bf16[8,128,256]{2,1,0:T(8,128)(2,1)}), bf16[8,128,256]{2,1,0:T(8,128)(2,1)S(1)}, u32[]{:S(2)}, u32[]{:S(2)}) async-start(bf16[8,128,256]{2,1,0:T(8,128)(2,1)} %get-tuple-element.13), calls=%async_computation | async-start | bytes 1048576 | tf_op jit(solution)/shard_map/all_to_all | solution.py:186
  39.8 0.2 select_convert_fusion.mask_ref
  40.0 0.0 collective-permute-done
  40.1 0.0 copy-start.2
  40.1 1.0 %copy-done.2 = bf16[1,128,4096]{2,1,0:T(8,128)(2,1)} copy-done((bf16[1,128,4096]{2,1,0:T(8,128)(2,1)}, bf16[1,128,4096]{2,1,0:T(8,128)(2,1)S(1)}, u32[]{:S(2)}) %copy-start.2) | copy-done | bytes 1048600
  41.0 3.6 %turn.1.query_ref = bf16[4096,128]{1,0:T(8,128)(2,1)} custom-call(bf16[128,4096]{1,0:T(8,128)(2,1)} %bitcast.8, f32[128,128]{1,0:T(8,128)} %get-tuple-element.11.cosine_ref, f32[128,128]{1,0:T(8,128)} %get-tuple-element.12.sine_ref), custom_call_target="tpu_custom_call" | custom-call | tf_op jit(solution)/shard_map/turn/pallas_call | solution.py:89
  44.7 0.0 copy-start
  44.7 1.2 %copy-done = bf16[4096,128]{1,0:T(8,128)(2,1)S(1)} copy-done((bf16[4096,128]{1,0:T(8,128)(2,1)S(1)}, bf16[4096,128]{1,0:T(8,128)(2,1)}, u32[]{:S(2)}) %copy-start) | copy-done | bytes 1048600
  45.9 0.0 copy-start.1
  45.9 3.5 %attend.2.rest_0_ = bf16[128,4096]{1,0:T(8,128)(2,1)} custom-call(bf16[4096,128]{1,0:T(8,128)(2,1)S(1)} %copy-done, bf16[8,128,256]{2,1,0:T(8,128)(2,1)S(1)} %all-to-all-done.1.gathered_ref, bf16[1024,128]{1,0:T(8,128)(2,1)S(1)} %select_convert_fusion.mask_ref), custom_call_target="tpu_custom_call" | custom-call | flops 2147483648 | bytes 1048576 | tf_op jit(solution)/shard_map/attend/pallas_call | solution.py:157
  49.4 8.3 %all-to-all-done.gathered_ref = bf16[8,128,256]{2,1,0:T(8,128)(2,1)S(1)} async-done(((bf16[8,128,256]{2,1,0:T(8,128)(2,1)}), bf16[8,128,256]{2,1,0:T(8,128)(2,1)S(1)}, u32[]{:S(2)}, u32[]{:S(2)}) %all-to-all-start) | async-done | bytes 524320 | tf_op jit(solution)/shard_map/all_to_all | solution.py:186
  57.7 0.0 copy-done.1
  57.7 3.5 %attend.3 = bf16[128,4096]{1,0:T(8,128)(2,1)} custom-call(bf16[4096,128]{1,0:T(8,128)(2,1)S(1)} %copy-done.1, bf16[8,128,256]{2,1,0:T(8,128)(2,1)S(1)} %all-to-all-done.gathered_ref, bf16[1024,128]{1,0:T(8,128)(2,1)S(1)} %select_convert_fusion.mask_ref, bf16[128,4096]{1,0:T(8,128)(2,1)} %attend.2.rest_0_), custom_call_target="tpu_custom_call", output_to_operand_aliasing={{}: (3, {})} | custom-call | flops 2147483648 | bytes 1048576 | tf_op jit(solution)/shard_map/attend/pallas_call | solution.py:157
  (2 shorter events, 0.0 us)
Async XLA Ops:
  0.0 5.6 %collective-permute-start.1 = (bf16[1,128,256]{2,1,0:T(8,128)(2,1)}, bf16[1,128,256]{2,1,0:T(8,128)(2,1)S(1)}, u32[]{:S(2)}, u32[]{:S(2)}) collective-permute-start(bf16[1,128,256]{2,1,0:T(8,128)(2,1)} %param.7), channel_id=1, source_target_pairs={{480,0},{0,32},{32,64},{64,96},{96,128},{128,160},{160,192},{192,2... | collective-permute-start | bytes 196616 | tf_op jit(solution)/shard_map/ppermute | solution.py:21
  3.1 2.5 %collective-permute-start.2 = (bf16[1,128,256]{2,1,0:T(8,128)(2,1)}, bf16[1,128,256]{2,1,0:T(8,128)(2,1)S(1)}, u32[]{:S(2)}, u32[]{:S(2)}) collective-permute-start(bf16[1,128,256]{2,1,0:T(8,128)(2,1)} %param.8), channel_id=1, source_target_pairs={{480,0},{0,32},{32,64},{64,96},{96,128},{128,160},{160,192},{192,2... | collective-permute-start | bytes 196616 | tf_op jit(solution)/shard_map/ppermute | solution.py:21
  3.1 0.7 %copy-start.5 = (s32[1,1024]{1,0:T(1,128)S(1)}, s32[1,1024]{1,0:T(1,128)}, u32[]{:S(2)}) copy-start(s32[1,1024]{1,0:T(1,128)} %param.9) | copy-start | bytes 12292
  3.8 0.7 %copy-start.6 = (f32[64]{0:T(128)S(1)}, f32[64]{0:T(128)}, u32[]{:S(2)}) copy-start(f32[64]{0:T(128)} %constant.47.clone) | copy-start | bytes 772
  3.8 0.7 %copy-start.7 = (f32[64]{0:T(128)S(1)}, f32[64]{0:T(128)}, u32[]{:S(2)}) copy-start(f32[64]{0:T(128)} %constant.46.clone) | copy-start | bytes 772
  3.8 14.5 %copy-start.8 = (bf16[1,128,4096]{2,1,0:T(8,128)(2,1)S(1)}, bf16[1,128,4096]{2,1,0:T(8,128)(2,1)}, u32[]{:S(2)}) copy-start(bf16[1,128,4096]{2,1,0:T(8,128)(2,1)} %param.6) | copy-start | bytes 3145732
  5.6 0.6 %copy-start.3 = (bf16[1,128,256]{2,1,0:T(8,128)(2,1)}, bf16[1,128,256]{2,1,0:T(8,128)(2,1)S(1)}, u32[]{:S(2)}) copy-start(bf16[1,128,256]{2,1,0:T(8,128)(2,1)S(1)} %collective-permute-done.1) | copy-start | bytes 196612
  5.6 0.6 %copy-start.4 = (bf16[1,128,256]{2,1,0:T(8,128)(2,1)}, bf16[1,128,256]{2,1,0:T(8,128)(2,1)S(1)}, u32[]{:S(2)}) copy-start(bf16[1,128,256]{2,1,0:T(8,128)(2,1)S(1)} %collective-permute-done.2) | copy-start | bytes 196612
  8.3 28.1 %all-to-all-start.1 = ((bf16[8,128,256]{2,1,0:T(8,128)(2,1)}), bf16[8,128,256]{2,1,0:T(8,128)(2,1)S(1)}, u32[]{:S(2)}, u32[]{:S(2)}) async-start(bf16[8,128,256]{2,1,0:T(8,128)(2,1)} %get-tuple-element.14), calls=%async_computation.1 | async-start | bytes 1048576 | tf_op jit(solution)/shard_map/all_to_all | solution.py:186
  18.4 21.7 %collective-permute-start = (bf16[1,128,4096]{2,1,0:T(8,128)(2,1)S(1)}, bf16[1,128,4096]{2,1,0:T(8,128)(2,1)S(1)}, u32[]{:S(2)}, u32[]{:S(2)}) collective-permute-start(bf16[1,128,4096]{2,1,0:T(8,128)(2,1)S(1)} %copy-done.8), channel_id=1, source_target_pairs={{480,0},{0,32},{32,64},{64,96},{96,128},{128,160},{160,192},{192,2... | collective-permute-start | bytes 3145736 | tf_op jit(solution)/shard_map/ppermute | solution.py:21
  36.3 21.4 %all-to-all-start = ((bf16[8,128,256]{2,1,0:T(8,128)(2,1)}), bf16[8,128,256]{2,1,0:T(8,128)(2,1)S(1)}, u32[]{:S(2)}, u32[]{:S(2)}) async-start(bf16[8,128,256]{2,1,0:T(8,128)(2,1)} %get-tuple-element.13), calls=%async_computation | async-start | bytes 1048576 | tf_op jit(solution)/shard_map/all_to_all | solution.py:186
  40.1 1.0 %copy-start.2 = (bf16[1,128,4096]{2,1,0:T(8,128)(2,1)}, bf16[1,128,4096]{2,1,0:T(8,128)(2,1)S(1)}, u32[]{:S(2)}) copy-start(bf16[1,128,4096]{2,1,0:T(8,128)(2,1)S(1)} %collective-permute-done) | copy-start | bytes 3145732
  44.7 1.2 %copy-start = (bf16[4096,128]{1,0:T(8,128)(2,1)S(1)}, bf16[4096,128]{1,0:T(8,128)(2,1)}, u32[]{:S(2)}) copy-start(bf16[4096,128]{1,0:T(8,128)(2,1)} %turn.1.query_ref) | copy-start | bytes 3145732
  45.9 11.8 %copy-start.1 = (bf16[4096,128]{1,0:T(8,128)(2,1)S(1)}, bf16[4096,128]{1,0:T(8,128)(2,1)}, u32[]{:S(2)}) copy-start(bf16[4096,128]{1,0:T(8,128)(2,1)} %turn.1.query_ref) | copy-start | bytes 3145732

commit v2 on v1

v2 whole, which is shorter than its diff:
```python
from functools import partial
import math

import jax
import jax.numpy as jnp
import numpy as np
from jax import lax
from jax.experimental import pallas as pl
from jax.experimental.pallas import tpu as pltpu
from jax.sharding import PartitionSpec as P

HEAD_DIM = 128
MASKED = -1e30
SCALE = math.log2(math.e) / math.sqrt(HEAD_DIM)
HEADS_PER_PASS = 2


def shifted(block, axis, distance):
    devices = range(lax.axis_size(axis))
    route = [((i - distance) % len(devices), i) for i in devices]
    return lax.ppermute(block, axis, route)


def rope_tables(head_size):
    index_ids = np.arange(head_size // 2) * 1.0
    natural = 500000.0 ** (-2.0 * index_ids / head_size)
    wavelength = 2.0 * math.pi / natural
    smooth = (8192.0 / wavelength - 1.0) / 3.0
    blended = (1.0 - smooth) * natural / 8.0 + smooth * natural
    scaled = np.where(
        wavelength < 2048.0, natural, np.where(wavelength > 8192.0, natural / 8.0, blended)
    )
    coarse = np.mod(1024.0 * scaled, 2.0 * math.pi)
    return (jnp.asarray(scaled, jnp.float32), jnp.asarray(coarse, jnp.float32))


def turn_tables(token_pos):
    fine_freq, coarse = rope_tables(HEAD_DIM)
    upper_part = (token_pos // 1024).astype(jnp.float32)
    lower_part = (token_pos % 1024).astype(jnp.float32)
    angles = upper_part[:, None] * coarse[None, :] + lower_part[:, None] * fine_freq[None, :]
    cosine, sine = jnp.cos(angles), jnp.sin(angles)
    return (
        jnp.concatenate([cosine, cosine], axis=-1),
        jnp.concatenate([-sine, sine], axis=-1),
    )


def turned(head, cosine, sine):
    head = head.astype(jnp.float32)
    return (head * cosine + pltpu.roll(head, HEAD_DIM // 2, 1) * sine).astype(jnp.bfloat16)


def spread_kernel(key_ref, value_ref, cosine_ref, sine_ref, out_ref):
    cosine, sine = cosine_ref[...], sine_ref[...]
    for head in range(key_ref.shape[1] // HEAD_DIM):
        columns = pl.ds(head * HEAD_DIM, HEAD_DIM)
        keys = turned(key_ref[:, columns], cosine, sine)
        values = value_ref[:, columns]
        for owner in range(out_ref.shape[0]):
            out_ref[owner, :, pl.ds(2 * head * HEAD_DIM, HEAD_DIM)] = keys
            out_ref[owner, :, pl.ds((2 * head + 1) * HEAD_DIM, HEAD_DIM)] = values


WHOLE = pl.BlockSpec(memory_space=pltpu.VMEM)


def spread(key_in, value_in, cosine, sine, owners):
    rows, width = key_in.shape
    return pl.pallas_call(
        spread_kernel,
        in_specs=[WHOLE] * 4,
        out_specs=WHOLE,
        out_shape=jax.ShapeDtypeStruct((owners, rows, 2 * width), jnp.bfloat16),
        name="spread",
    )(key_in, value_in, cosine, sine)


def turn_kernel(query_ref, cosine_ref, sine_ref, out_ref):
    cosine, sine = cosine_ref[...], sine_ref[...]
    rows = query_ref.shape[0]
    for head in range(query_ref.shape[1] // HEAD_DIM):
        out_ref[head * rows : (head + 1) * rows, :] = turned(
            query_ref[:, head * HEAD_DIM : (head + 1) * HEAD_DIM], cosine, sine
        )


def turn_queries(query_in, cosine, sine):
    rows, width = query_in.shape
    heads = width // HEAD_DIM
    return pl.pallas_call(
        turn_kernel,
        in_specs=[WHOLE] * 3,
        out_specs=WHOLE,
        out_shape=jax.ShapeDtypeStruct((heads * rows, HEAD_DIM), jnp.bfloat16),
        name="turn",
    )(query_in, cosine, sine)


def attend_kernel(raw_ref, cosine_ref, sine_ref, gathered_ref, mask_ref, out_ref, held_ref, query_ref, sent):
    turn_kernel(raw_ref, cosine_ref, sine_ref, query_ref)
    tokens, rows = mask_ref.shape
    key_heads = gathered_ref.shape[2] // (2 * HEAD_DIM)
    size = HEADS_PER_PASS * rows
    per_head = query_ref.shape[0] // key_heads
    own = lax.broadcasted_iota(jnp.int32, (size, rows), 0) % rows
    one_hot = (own == lax.broadcasted_iota(jnp.int32, (size, rows), 1)).astype(jnp.bfloat16)
    mask = mask_ref[...]
    ones = jnp.ones((tokens, HEAD_DIM), jnp.bfloat16)

    def part(index):
        piece = gathered_ref[:, :, index * HEAD_DIM : (index + 1) * HEAD_DIM]
        return piece.reshape(tokens, HEAD_DIM)

    def score(keys, step):
        queries = jnp.concatenate([query_ref[step * size : (step + 1) * size, :], one_hot], axis=1)
        return lax.dot_general(
            queries, keys, (((1,), (1,)), ((), ())), preferred_element_type=jnp.float32
        )

    copies = []
    steps = per_head // size
    for key_head in range(key_heads):
        keys = jnp.concatenate([part(2 * key_head), mask], axis=1)
        values = jnp.concatenate([part(2 * key_head + 1), ones], axis=1)
        following = score(keys, key_head * steps)
        for step in range(key_head * steps, (key_head + 1) * steps):
            scores = following
            if step + 1 < (key_head + 1) * steps:
                following = score(keys, step + 1)
            highest = jnp.max(scores, axis=-1, keepdims=True)
            weights = jnp.exp2((scores - highest) * SCALE).astype(jnp.bfloat16)
            summed = lax.dot_general(
                weights, values, (((1,), (0,)), ((), ())), preferred_element_type=jnp.float32
            )
            attended = (summed[:, :HEAD_DIM] / summed[:, HEAD_DIM:]).astype(jnp.bfloat16)
            for i in range(HEADS_PER_PASS):
                head = step * HEADS_PER_PASS + i
                held_ref[:, head * HEAD_DIM : (head + 1) * HEAD_DIM] = attended[
                    i * rows : (i + 1) * rows
                ]
            columns = pl.ds(step * HEADS_PER_PASS * HEAD_DIM, HEADS_PER_PASS * HEAD_DIM)
            copies.append(
                pltpu.make_async_copy(held_ref.at[:, columns], out_ref.at[:, columns], sent.at[step])
            )
            copies[-1].start()
    for copy in copies:
        copy.wait()


def attend(queries, cosine, sine, gathered, mask):
    tokens, rows = mask.shape
    heads = queries.shape[1] // HEAD_DIM
    return pl.pallas_call(
        attend_kernel,
        in_specs=[WHOLE] * 5,
        out_specs=pl.BlockSpec(memory_space=pl.ANY),
        out_shape=jax.ShapeDtypeStruct((rows, heads * HEAD_DIM), jnp.bfloat16),
        scratch_shapes=[
            pltpu.VMEM((rows, heads * HEAD_DIM), jnp.bfloat16),
            pltpu.VMEM((rows * heads, HEAD_DIM), jnp.bfloat16),
            pltpu.SemaphoreType.DMA((heads // HEADS_PER_PASS,)),
        ],
        compiler_params=pltpu.CompilerParams(vmem_limit_bytes=40 * 1024 * 1024),
        cost_estimate=pl.CostEstimate(
            flops=8 * heads * rows * tokens * HEAD_DIM,
            bytes_accessed=4 * heads * rows * HEAD_DIM,
            transcendentals=heads * rows * tokens,
        ),
        name="attend",
    )(queries, cosine, sine, gathered, mask)


def per_device(query_rows, key_rows, value_rows, positions):
    local_rows = query_rows.shape[1]
    key_heads = key_rows.shape[2] // HEAD_DIM
    owners = lax.axis_size("ctx")
    key_in, value_in = shifted((key_rows, value_rows), "section", 1)
    position_table = positions[0]
    own_pos = lax.dynamic_slice_in_dim(
        position_table, lax.axis_index("ctx") * local_rows, local_rows
    )
    cosine, sine = turn_tables(own_pos)
    mask = jnp.where(position_table[:, None] <= own_pos[None, :], 0.0, MASKED).astype(jnp.bfloat16)
    query_rows, own_pos = lax.optimization_barrier((query_rows, own_pos))
    query_in = shifted(query_rows, "section", 1)
    spread_rows = spread(key_in[0], value_in[0], cosine, sine, owners)
    gathered = lax.all_to_all(spread_rows, "ctx", 0, 0, tiled=False)
    return attend(query_in[0], cosine, sine, gathered, mask)[None]


def solution(mesh):
    return jax.shard_map(
        per_device,
        mesh=mesh,
        in_specs=(
            P("section", "ctx", "tp"),
            P("section", "ctx", "tp"),
            P("section", "ctx", "tp"),
            P("section", None),
        ),
        out_specs=P("section", "ctx", "tp"),
        check_vma=False,
    )
```

time: 61.7 us -> 54.4 us (0.88)
  Pallas kernels: 12.7 us -> 8.43 us
  starting transfers between devices: 20.3 us -> 16.9 us
  waiting for transfers between devices: 22.7 us -> 25.5 us
  local copies, waits for them, and re-layouts: 4.17 us -> 1.99 us
    ppermute x3, waiting for transfers between devices: 0.01 us -> 11.5 us  [shifted(): return lax.ppermute(block, axis, route)]
    all_to_all x2 -> x1, waiting for transfers between devices: 22.7 us -> 13.9 us  [per_device(): gathered = lax.all_to_all(spread_rows, 'ctx', 0, 0, tiled=False)]
    pallas_call x4 -> x2, Pallas kernels: 12.7 us -> 8.43 us  [the longest x1 6.36 us: attend(): pl.pallas_call(attend_kernel, in_specs=[WHOLE] * 5, out_specs=pl.BlockSpe...]
    all_to_all x2 -> x1, starting transfers between devices: 13.6 us -> 10.2 us  [per_device(): gathered = lax.all_to_all(spread_rows, 'ctx', 0, 0, tiled=False)]
    unnamed x18 -> x16, local copies, waits for them, and re-layouts: 4.17 us -> 1.99 us
  transfers between devices with their start and end apart: 5 -> 4, of which waited for: 2 -> 2; matrix products, arithmetic and copies ran while one was open for 2% -> 2% of each run, Pallas kernels for 12% -> 0%
where the time goes in v2:
time: 54.4 us; the launch traced here: 54.2 us
  waiting for transfers between devices  25.5 us (47%)
  starting transfers between devices  16.9 us (31%)
  Pallas kernels  8.43 us (15%)
  local copies, waits for them, and re-layouts  1.99 us (4%)
  other arithmetic  1.31 us (2%)
    all_to_all x1, waiting for transfers between devices, per_device(): gathered = lax.all_to_all(spread_rows, 'ctx', 0, 0, tiled=False)  13.9 us
    ppermute x3, waiting for transfers between devices, shifted(): return lax.ppermute(block, axis, route)  11.5 us
    all_to_all x1, starting transfers between devices, per_device(): gathered = lax.all_to_all(spread_rows, 'ctx', 0, 0, tiled=False)  10.2 us
    ppermute x3, starting transfers between devices, shifted(): return lax.ppermute(block, axis, route)  6.65 us
    pallas_call x1, Pallas kernels, attend(): pl.pallas_call(attend_kernel, in_specs=[WHOLE] * 5, out_specs=pl.BlockSpe...  6.36 us
    pallas_call x1, Pallas kernels, spread(): pl.pallas_call(spread_kernel, in_specs=[WHOLE] * 4, out_specs=WHOLE, out_...  2.07 us
    unnamed x16, local copies, waits for them, and re-layouts  1.99 us
  transfers between devices with their start and end apart: 4, of which 2 were waited for; matrix products, arithmetic and copies ran while one was open for 2% of the time, Pallas kernels for 0%

profile of v2, /device:TPU:27, one launch (start us, length us, event | category | flops | bytes accessed | tf_op | source)
XLA Modules:
  0.0 54.2 jit_solution(11409688722470802322)
XLA Ops:
  0.0 3.1 %collective-permute-start.1 = (bf16[1,128,256]{2,1,0:T(8,128)(2,1)}, bf16[1,128,256]{2,1,0:T(8,128)(2,1)S(1)}, u32[]{:S(2)}, u32[]{:S(2)}) collective-permute-start(bf16[1,128,256]{2,1,0:T(8,128)(2,1)} %param.7), channel_id=1, source_target_pairs={{480,0},{0,32},{32,64},{64,96},{96,128},{128,160},{160,192},{192,2... | collective-permute-start | bytes 196616 | tf_op jit(solution)/shard_map/ppermute | solution.py:21
  3.1 0.0 collective-permute-start.2
  3.1 0.0 copy-start.4
  3.1 0.7 %copy-done.4 = s32[1,1024]{1,0:T(1,128)S(1)} copy-done((s32[1,1024]{1,0:T(1,128)S(1)}, s32[1,1024]{1,0:T(1,128)}, u32[]{:S(2)}) %copy-start.4) | copy-done | bytes 4120
  3.8 0.0 copy-start.5
  3.8 0.0 copy-start.6
  3.8 0.6 %copy-done.5 = f32[64]{0:T(128)S(1)} copy-done((f32[64]{0:T(128)S(1)}, f32[64]{0:T(128)}, u32[]{:S(2)}) %copy-start.5) | copy-done | bytes 280
  4.5 0.0 copy-done.6
  4.5 0.3 fusion.2
  4.8 0.8 %pad_maximum_fusion = (f32[128,128]{1,0:T(8,128)}, f32[128,128]{1,0:T(8,128)}) fusion(f32[128,64]{1,0:T(8,128)S(1)} %get-tuple-element.9, f32[128,64]{1,0:T(8,128)S(1)} %get-tuple-element.8, f32[128,64]{1,0:T(8,128)S(1)} %get-tuple-element.7), kind=kLoop, calls=%fused_computation.1 | loop fusion | flops 32768 | bytes 229376 | tf_op jit(solution)/shard_map/concatenate | solution.py:44
  5.6 0.0 collective-permute-done.1
  5.6 0.0 copy-start.2
  5.6 0.0 collective-permute-done.2
  5.6 0.0 copy-start.3
  5.6 0.6 %copy-done.2 = bf16[1,128,256]{2,1,0:T(8,128)(2,1)} copy-done((bf16[1,128,256]{2,1,0:T(8,128)(2,1)}, bf16[1,128,256]{2,1,0:T(8,128)(2,1)S(1)}, u32[]{:S(2)}) %copy-start.2) | copy-done | bytes 65560
  6.2 0.0 copy-done.3
  6.2 2.1 %spread.1 = bf16[8,128,512]{2,1,0:T(8,128)(2,1)} custom-call(bf16[128,256]{1,0:T(8,128)(2,1)} %bitcast.9, bf16[128,256]{1,0:T(8,128)(2,1)} %bitcast.10, f32[128,128]{1,0:T(8,128)} %get-tuple-element.10.cosine_ref, f32[128,128]{1,0:T(8,128)} %get-tuple-element.11.sine_ref), custom_call_target="tpu_custom_call" | custom-call | tf_op jit(solution)/shard_map/spread/pallas_call | solution.py:70
  8.3 0.0 copy-start.7
  8.3 10.2 %all-to-all-start = ((bf16[8,128,512]{2,1,0:T(8,128)(2,1)}), bf16[8,128,512]{2,1,0:T(8,128)(2,1)S(1)}, u32[]{:S(2)}, u32[]{:S(2)}) async-start(bf16[8,128,512]{2,1,0:T(8,128)(2,1)} %spread.1), calls=%async_computation | async-start | bytes 2097152 | tf_op jit(solution)/shard_map/all_to_all | solution.py:188
  18.6 0.0 copy-done.7
  18.6 3.5 %collective-permute-start = (bf16[1,128,4096]{2,1,0:T(8,128)(2,1)S(1)}, bf16[1,128,4096]{2,1,0:T(8,128)(2,1)S(1)}, u32[]{:S(2)}, u32[]{:S(2)}) collective-permute-start(bf16[1,128,4096]{2,1,0:T(8,128)(2,1)S(1)} %copy-done.7), channel_id=1, source_target_pairs={{480,0},{0,32},{32,64},{64,96},{96,128},{128,160},{160,192},{192,2... | collective-permute-start | bytes 3145736 | tf_op jit(solution)/shard_map/ppermute | solution.py:21
  22.1 0.0 copy-start
  22.1 0.0 copy-start.1
  22.1 0.2 select_convert_fusion.mask_ref
  22.3 11.5 %collective-permute-done = bf16[1,128,4096]{2,1,0:T(8,128)(2,1)S(1)} collective-permute-done((bf16[1,128,4096]{2,1,0:T(8,128)(2,1)S(1)}, bf16[1,128,4096]{2,1,0:T(8,128)(2,1)S(1)}, u32[]{:S(2)}, u32[]{:S(2)}) %collective-permute-start) | collective-permute-done | bytes 1048608 | tf_op jit(solution)/shard_map/ppermute | solution.py:21
  33.9 13.9 %all-to-all-done.gathered_ref = bf16[8,128,512]{2,1,0:T(8,128)(2,1)S(1)} async-done(((bf16[8,128,512]{2,1,0:T(8,128)(2,1)}), bf16[8,128,512]{2,1,0:T(8,128)(2,1)S(1)}, u32[]{:S(2)}, u32[]{:S(2)}) %all-to-all-start) | async-done | bytes 1048608 | tf_op jit(solution)/shard_map/all_to_all | solution.py:188
  47.8 0.0 copy-done
  47.8 0.0 copy-done.1
  47.8 6.4 %attend.1 = bf16[128,4096]{1,0:T(8,128)(2,1)} custom-call(bf16[128,4096]{1,0:T(8,128)(2,1)S(1)} %bitcast.8, f32[128,128]{1,0:T(8,128)S(1)} %copy-done, f32[128,128]{1,0:T(8,128)S(1)} %copy-done.1, bf16[8,128,512]{2,1,0:T(8,128)(2,1)S(1)} %all-to-all-done.gathered_ref, bf16[1024,128]{1,0:T(8,128)(2,1)S(1)} %select_convert_fusion.mask_ref), custom_call_target="tpu_custom_call" | custom-call | flops 4294967296 | bytes 2097152 | tf_op jit(solution)/shard_map/attend/pallas_call | solution.py:154
  (2 shorter events, 0.0 us)
Async XLA Ops:
  0.0 5.6 %collective-permute-start.1 = (bf16[1,128,256]{2,1,0:T(8,128)(2,1)}, bf16[1,128,256]{2,1,0:T(8,128)(2,1)S(1)}, u32[]{:S(2)}, u32[]{:S(2)}) collective-permute-start(bf16[1,128,256]{2,1,0:T(8,128)(2,1)} %param.7), channel_id=1, source_target_pairs={{480,0},{0,32},{32,64},{64,96},{96,128},{128,160},{160,192},{192,2... | collective-permute-start | bytes 196616 | tf_op jit(solution)/shard_map/ppermute | solution.py:21
  3.1 2.5 %collective-permute-start.2 = (bf16[1,128,256]{2,1,0:T(8,128)(2,1)}, bf16[1,128,256]{2,1,0:T(8,128)(2,1)S(1)}, u32[]{:S(2)}, u32[]{:S(2)}) collective-permute-start(bf16[1,128,256]{2,1,0:T(8,128)(2,1)} %param.8), channel_id=1, source_target_pairs={{480,0},{0,32},{32,64},{64,96},{96,128},{128,160},{160,192},{192,2... | collective-permute-start | bytes 196616 | tf_op jit(solution)/shard_map/ppermute | solution.py:21
  3.1 0.7 %copy-start.4 = (s32[1,1024]{1,0:T(1,128)S(1)}, s32[1,1024]{1,0:T(1,128)}, u32[]{:S(2)}) copy-start(s32[1,1024]{1,0:T(1,128)} %param.9) | copy-start | bytes 12292
  3.8 0.7 %copy-start.5 = (f32[64]{0:T(128)S(1)}, f32[64]{0:T(128)}, u32[]{:S(2)}) copy-start(f32[64]{0:T(128)} %constant.47.clone) | copy-start | bytes 772
  3.8 0.7 %copy-start.6 = (f32[64]{0:T(128)S(1)}, f32[64]{0:T(128)}, u32[]{:S(2)}) copy-start(f32[64]{0:T(128)} %constant.46.clone) | copy-start | bytes 772
  5.6 0.6 %copy-start.2 = (bf16[1,128,256]{2,1,0:T(8,128)(2,1)}, bf16[1,128,256]{2,1,0:T(8,128)(2,1)S(1)}, u32[]{:S(2)}) copy-start(bf16[1,128,256]{2,1,0:T(8,128)(2,1)S(1)} %collective-permute-done.1) | copy-start | bytes 196612
  5.6 0.6 %copy-start.3 = (bf16[1,128,256]{2,1,0:T(8,128)(2,1)}, bf16[1,128,256]{2,1,0:T(8,128)(2,1)S(1)}, u32[]{:S(2)}) copy-start(bf16[1,128,256]{2,1,0:T(8,128)(2,1)S(1)} %collective-permute-done.2) | copy-start | bytes 196612
  8.3 10.2 %copy-start.7 = (bf16[1,128,4096]{2,1,0:T(8,128)(2,1)S(1)}, bf16[1,128,4096]{2,1,0:T(8,128)(2,1)}, u32[]{:S(2)}) copy-start(bf16[1,128,4096]{2,1,0:T(8,128)(2,1)} %param.6) | copy-start | bytes 3145732
  8.3 39.5 %all-to-all-start = ((bf16[8,128,512]{2,1,0:T(8,128)(2,1)}), bf16[8,128,512]{2,1,0:T(8,128)(2,1)S(1)}, u32[]{:S(2)}, u32[]{:S(2)}) async-start(bf16[8,128,512]{2,1,0:T(8,128)(2,1)} %spread.1), calls=%async_computation | async-start | bytes 2097152 | tf_op jit(solution)/shard_map/all_to_all | solution.py:188
  18.6 15.3 %collective-permute-start = (bf16[1,128,4096]{2,1,0:T(8,128)(2,1)S(1)}, bf16[1,128,4096]{2,1,0:T(8,128)(2,1)S(1)}, u32[]{:S(2)}, u32[]{:S(2)}) collective-permute-start(bf16[1,128,4096]{2,1,0:T(8,128)(2,1)S(1)} %copy-done.7), channel_id=1, source_target_pairs={{480,0},{0,32},{32,64},{64,96},{96,128},{128,160},{160,192},{192,2... | collective-permute-start | bytes 3145736 | tf_op jit(solution)/shard_map/ppermute | solution.py:21
  22.1 25.7 %copy-start = (f32[128,128]{1,0:T(8,128)S(1)}, f32[128,128]{1,0:T(8,128)}, u32[]{:S(2)}) copy-start(f32[128,128]{1,0:T(8,128)} %get-tuple-element.10.cosine_ref) | copy-start | bytes 196612
  22.1 25.7 %copy-start.1 = (f32[128,128]{1,0:T(8,128)S(1)}, f32[128,128]{1,0:T(8,128)}, u32[]{:S(2)}) copy-start(f32[128,128]{1,0:T(8,128)} %get-tuple-element.11.sine_ref) | copy-start | bytes 196612

commit v3 on v2

v3 whole, which is shorter than its diff:
```python
from functools import partial
import math

import jax
import jax.numpy as jnp
import numpy as np
from jax import lax
from jax.experimental import pallas as pl
from jax.experimental.pallas import tpu as pltpu
from jax.sharding import PartitionSpec as P

HEAD_DIM = 128
MASKED = -1e30
SCALE = math.log2(math.e) / math.sqrt(HEAD_DIM)
HEADS_PER_PASS = 4
GROUPS = ((0, 1, 2), (3,))


def shifted(block, axis, distance):
    devices = range(lax.axis_size(axis))
    route = [((i - distance) % len(devices), i) for i in devices]
    return lax.ppermute(block, axis, route)


def rope_tables():
    index_ids = np.arange(HEAD_DIM // 2) * 1.0
    natural = 500000.0 ** (-2.0 * index_ids / HEAD_DIM)
    wavelength = 2.0 * math.pi / natural
    smooth = (8192.0 / wavelength - 1.0) / 3.0
    blended = (1.0 - smooth) * natural / 8.0 + smooth * natural
    scaled = np.where(
        wavelength < 2048.0, natural, np.where(wavelength > 8192.0, natural / 8.0, blended)
    )
    coarse = np.mod(1024.0 * scaled, 2.0 * math.pi)
    sign = np.repeat(np.array([-1.0, 1.0]), HEAD_DIM // 2)
    return [jnp.asarray(table, jnp.float32) for table in (np.tile(scaled, 2), np.tile(coarse, 2), sign)]


def turn_tables(token_pos):
    fine, coarse, sign = rope_tables()
    upper_part = (token_pos // 1024).astype(jnp.float32)
    lower_part = (token_pos % 1024).astype(jnp.float32)
    angles = upper_part[:, None] * coarse[None, :] + lower_part[:, None] * fine[None, :]
    return jnp.cos(angles), jnp.sin(angles) * sign[None, :]


def turned(head, cosine, sine):
    head = head.astype(jnp.float32)
    return (head * cosine + pltpu.roll(head, HEAD_DIM // 2, 1) * sine).astype(jnp.bfloat16)


def turned_rows(rows, cosine, sine):
    half = rows.shape[1] // 2
    heads = [turned(rows[:, i : i + HEAD_DIM], cosine, sine) for i in range(0, half, HEAD_DIM)]
    return jnp.concatenate(heads + [rows[:, half:]], axis=1)


def turn_pair_kernel(own_ref, partner_ref, cosine_ref, sine_ref, out_ref):
    count = own_ref.shape[0]
    for i, ref in enumerate((own_ref, partner_ref)):
        place = pl.ds(i * count, count)
        out_ref[place] = turned_rows(ref[...], cosine_ref[place], sine_ref[place])


WHOLE = pl.BlockSpec(memory_space=pltpu.VMEM)
SMALL = pltpu.CompilerParams(vmem_limit_bytes=8 * 1024 * 1024)


def turn_pair(own_rows, partner_rows, cosine, sine):
    rows, width = own_rows.shape
    return pl.pallas_call(
        turn_pair_kernel,
        in_specs=[WHOLE] * 4,
        out_specs=WHOLE,
        out_shape=jax.ShapeDtypeStruct((2 * rows, width), jnp.bfloat16),
        compiler_params=SMALL,
        name="turn_pair",
    )(own_rows, partner_rows, cosine, sine)


def turn_kernel(query_ref, cosine_ref, sine_ref, out_ref):
    rows = query_ref.shape[0]
    cosine, sine = cosine_ref[:rows], sine_ref[:rows]
    for head in range(query_ref.shape[1] // HEAD_DIM):
        out_ref[head * rows : (head + 1) * rows, :] = turned(
            query_ref[:, head * HEAD_DIM : (head + 1) * HEAD_DIM], cosine, sine
        )


def turn_queries(query_in, cosine, sine):
    rows, width = query_in.shape
    heads = width // HEAD_DIM
    return pl.pallas_call(
        turn_kernel,
        in_specs=[WHOLE] * 3,
        out_specs=WHOLE,
        out_shape=jax.ShapeDtypeStruct((heads * rows, HEAD_DIM), jnp.bfloat16),
        compiler_params=pltpu.CompilerParams(vmem_limit_bytes=8 * 1024 * 1024),
        name="turn",
    )(query_in, cosine, sine)


def attend_kernel(*refs, pieces, first, last):
    refs = list(refs)
    query_ref, *piece_refs = refs[: 1 + pieces]
    mask_ref = refs[1 + pieces]
    refs = refs[2 + pieces :]
    if not first:
        before_ref, before_highest_ref = refs[:2]
        refs = refs[2:]
    if last:
        out_ref, held_ref, sent = refs
    else:
        sums_ref, highest_ref = refs
    tokens, rows = mask_ref.shape
    key_heads = piece_refs[0].shape[1] // (2 * HEAD_DIM)
    size = HEADS_PER_PASS * rows
    steps = query_ref.shape[0] // key_heads // size
    own = lax.broadcasted_iota(jnp.int32, (size, rows), 0) % rows
    one_hot = (own == lax.broadcasted_iota(jnp.int32, (size, rows), 1)).astype(jnp.bfloat16)
    mask = mask_ref[...]
    ones = jnp.ones((tokens, HEAD_DIM), jnp.bfloat16)

    def part(index):
        columns = pl.ds(index * HEAD_DIM, HEAD_DIM)
        return jnp.concatenate([ref[:, columns] for ref in piece_refs], axis=0)

    def score(keys, step):
        queries = jnp.concatenate([query_ref[step * size : (step + 1) * size, :], one_hot], axis=1)
        return lax.dot_general(
            queries, keys, (((1,), (1,)), ((), ())), preferred_element_type=jnp.float32
        )

    copies = []
    for key_head in range(key_heads):
        keys = jnp.concatenate([part(key_head), mask], axis=1)
        values = jnp.concatenate([part(key_heads + key_head), ones], axis=1)
        following = score(keys, key_head * steps)
        for step in range(key_head * steps, (key_head + 1) * steps):
            place = pl.ds(step * size, size)
            scores = following
            if step + 1 < (key_head + 1) * steps:
                following = score(keys, step + 1)
            highest = jnp.max(scores, axis=-1, keepdims=True)
            if not first:
                before = before_highest_ref[place][:, :1]
                highest = jnp.maximum(highest, before)
            weights = jnp.exp2((scores - highest) * SCALE).astype(jnp.bfloat16)
            summed = lax.dot_general(
                weights, values, (((1,), (0,)), ((), ())), preferred_element_type=jnp.float32
            )
            if not first:
                summed = summed + before_ref[place] * jnp.exp2((before - highest) * SCALE)
            if not last:
                sums_ref[place] = summed
                highest_ref[place] = jnp.broadcast_to(highest, (size, HEAD_DIM))
                continue
            attended = (summed[:, :HEAD_DIM] / summed[:, HEAD_DIM:]).astype(jnp.bfloat16)
            for i in range(HEADS_PER_PASS):
                head = step * HEADS_PER_PASS + i
                held_ref[:, head * HEAD_DIM : (head + 1) * HEAD_DIM] = attended[
                    i * rows : (i + 1) * rows
                ]
            columns = pl.ds(step * HEADS_PER_PASS * HEAD_DIM, HEADS_PER_PASS * HEAD_DIM)
            copies.append(
                pltpu.make_async_copy(held_ref.at[:, columns], out_ref.at[:, columns], sent.at[step])
            )
            copies[-1].start()
    for copy in copies:
        copy.wait()


def attend(queries, pieces, mask, carried, last):
    tokens, rows = mask.shape
    count = queries.shape[0]
    heads = count // rows
    if last:
        out_specs = pl.BlockSpec(memory_space=pl.ANY)
        out_shape = jax.ShapeDtypeStruct((rows, heads * HEAD_DIM), jnp.bfloat16)
        scratch = [
            pltpu.VMEM((rows, heads * HEAD_DIM), jnp.bfloat16),
            pltpu.SemaphoreType.DMA((heads // HEADS_PER_PASS,)),
        ]
    else:
        out_specs = [WHOLE] * 2
        out_shape = [
            jax.ShapeDtypeStruct((count, 2 * HEAD_DIM), jnp.float32),
            jax.ShapeDtypeStruct((count, HEAD_DIM), jnp.float32),
        ]
        scratch = []
    operands = [queries, *pieces, mask, *carried]
    return pl.pallas_call(
        partial(attend_kernel, pieces=len(pieces), first=not carried, last=last),
        in_specs=[WHOLE] * len(operands),
        out_specs=out_specs,
        out_shape=out_shape,
        scratch_shapes=scratch,
        compiler_params=pltpu.CompilerParams(vmem_limit_bytes=24 * 1024 * 1024),
        cost_estimate=pl.CostEstimate(flops=1000, bytes_accessed=1000, transcendentals=0),
        name="attend",
    )(*operands)


def per_device(query_rows, key_rows, value_rows, positions):
    local_rows = query_rows.shape[1]
    sections, owners = lax.axis_size("section"), lax.axis_size("ctx")
    rows = jnp.concatenate([key_rows[0], value_rows[0]], axis=1)
    own_rows = shifted(rows, "section", 1)
    partner_rows = lax.ppermute(
        rows,
        ("section", "ctx"),
        [
            ((s - 1) % sections * owners + (c ^ 1), s * owners + c)
            for s in range(sections)
            for c in range(owners)
        ],
    )
    owner_index = lax.axis_index("ctx")
    blocks = positions[0].reshape(owners, local_rows)

    def pair_pos(index):
        return [lax.dynamic_index_in_dim(blocks, i, keepdims=False) for i in (index, index ^ 1)]

    def beside(index, hop):
        return (index + (1 - index % 2 * 2) * hop) % owners

    def route(hop):
        return [(beside(c, hop), c) for c in range(owners)]

    key_pos = [pair_pos(beside(owner_index, hop)) for hop in (0, 2, -1, -3)]
    own_pos = key_pos[0][0]
    cosine, sine = turn_tables(jnp.concatenate(key_pos[0]))
    masks = [
        jnp.where(jnp.concatenate(pos)[:, None] <= own_pos[None, :], 0.0, MASKED).astype(jnp.bfloat16)
        for pos in key_pos
    ]
    pair_rows = turn_pair(own_rows, partner_rows, cosine, sine)
    query_rows, pair_rows = lax.optimization_barrier((query_rows, pair_rows))
    query_in = shifted(query_rows, "section", 1)
    second = lax.ppermute(pair_rows, "ctx", route(2))
    beside_rows = lax.ppermute(pair_rows, "ctx", route(-1))
    across = lax.ppermute(second, "ctx", route(-1))
    queries = turn_queries(query_in[0], cosine, sine)
    carried = ()
    for i, pieces in enumerate(GROUPS):
        last = i + 1 == len(GROUPS)
        arrived = [(pair_rows, second, beside_rows, across)[p] for p in pieces]
        mask = jnp.concatenate([masks[p] for p in pieces], axis=0)
        carried = attend(queries, arrived, mask, carried, last)
    return carried[None]


def solution(mesh):
    return jax.shard_map(
        per_device,
        mesh=mesh,
        in_specs=(
            P("section", "ctx", "tp"),
            P("section", "ctx", "tp"),
            P("section", "ctx", "tp"),
            P("section", None),
        ),
        out_specs=P("section", "ctx", "tp"),
        check_vma=False,
    )
```

time: 54.4 us -> 44.4 us (0.82)
  the two profiles are of different devices: /device:TPU:27 before, /device:TPU:1 now
where the time goes in v3:
time: 44.4 us; the launch traced here: 43.6 us
  starting transfers between devices  24.7 us (56%)
  Pallas kernels  8.32 us (19%)
  waiting for transfers between devices  7.04 us (16%)
  other arithmetic  2.39 us (5%)
  local copies, waits for them, and re-layouts  1 us (2%)
    ppermute x1, starting transfers between devices, per_device(): second = lax.ppermute(pair_rows, 'ctx', route(2))  9.75 us
    pallas_call x2, Pallas kernels, attend(): pl.pallas_call(partial(attend_kernel, pieces=len(pieces), first=not carri...  7.71 us
    ppermute x1, starting transfers between devices, per_device(): lax.ppermute(rows, ('section', 'ctx'), [((s - 1) % sections * owners + (c...  6.4 us
    ppermute x1, starting transfers between devices, per_device(): across = lax.ppermute(second, 'ctx', route(-1))  4.08 us
    ppermute x1, waiting for transfers between devices, per_device(): second = lax.ppermute(pair_rows, 'ctx', route(2))  3.77 us
    ppermute x2, starting transfers between devices, shifted(): return lax.ppermute(block, axis, route)  2.51 us
    ppermute x1, starting transfers between devices, per_device(): beside_rows = lax.ppermute(pair_rows, 'ctx', route(-1))  1.92 us
    ppermute x1, waiting for transfers between devices, per_device(): across = lax.ppermute(second, 'ctx', route(-1))  1.58 us
  transfers between devices with their start and end apart: 6, of which 4 were waited for; matrix products, arithmetic and copies ran while one was open for 6% of the time, Pallas kernels for 10%

profile of v3, /device:TPU:1, one launch (start us, length us, event | category | flops | bytes accessed | tf_op | source)
XLA Modules:
  0.0 43.6 jit_solution(11758548952997004503)
XLA Ops:
  0.0 0.9 %pad_maximum_fusion.1 = bf16[128,512]{1,0:T(8,128)(2,1)S(1)} fusion(bf16[128,256]{1,0:T(8,128)(2,1)} %bitcast.22, bf16[128,256]{1,0:T(8,128)(2,1)} %bitcast.23), kind=kLoop, calls=%fused_computation.1 | loop fusion | flops 262144 | bytes 262144 | tf_op jit(solution)/shard_map/concatenate | solution.py:207
  0.9 6.4 %collective-permute-start.1 = (bf16[128,512]{1,0:T(8,128)(2,1)S(1)}, bf16[128,512]{1,0:T(8,128)(2,1)S(1)}, u32[]{:S(2)}, u32[]{:S(2)}) collective-permute-start(bf16[128,512]{1,0:T(8,128)(2,1)S(1)} %pad_maximum_fusion.1), channel_id=1, source_target_pairs={{484,0},{480,4},{492,8},{488,12},{500,16},{496,20},{508,24},{504,2... | collective-permute-start | bytes 393224 | tf_op jit(solution)/shard_map/ppermute | solution.py:209
  7.3 0.0 collective-permute-start
  7.4 1.0 %fusion.7 = (s32[128]{0:T(128)S(1)}, s32[128]{0:T(128)S(1)}, s32[128]{0:T(128)S(1)}, s32[128]{0:T(128)S(1)}, s32[128]{0:T(128)S(1)}, /*index=5*/s32[128]{0:T(128)S(1)}, s32[128]{0:T(128)S(1)}, s32[128]{0:T(128)S(1)}) fusion(s32[8,128]{1,0:T(8,128)} %bitcast.24, s32[]{:T(128)S(6)} %select_n.96, s32[]{:T(128)S(6)} %select_n.101, s32[]{:T(128)S(6)} %select_n.100, ...), kind=kLoop, calls=%fused_computation.32 | loop fusion | bytes 8224 | tf_op jit(solution)/shard_map/jit(dynamic_index_in_dim)/squeeze | solution.py:222
  8.4 1.3 %sine_multiply_fusion = (f32[256,128]{1,0:T(8,128)S(1)}, f32[256,128]{1,0:T(8,128)S(1)}) fusion(f32[128]{0:T(128)} %constant.105.clone, f32[128]{0:T(128)} %constant.103.clone, f32[256]{0:T(256)S(1)} %get-tuple-element.25, f32[128]{0:T(128)} %constant.104.clone, f32[256]{0:T(256)S(1)} %get-tuple-element.24), kind=kLoop, calls=%fused_computation.6 | loop fusion | flops 131072 | bytes 265728 | tf_op jit(solution)/shard_map/mul | solution.py:44
  9.7 0.0 collective-permute-done.1.partner_ref
  9.7 0.9 %collective-permute-done.own_ref = bf16[128,512]{1,0:T(8,128)(2,1)S(1)} collective-permute-done((bf16[128,512]{1,0:T(8,128)(2,1)S(1)}, bf16[128,512]{1,0:T(8,128)(2,1)S(1)}, u32[]{:S(2)}, u32[]{:S(2)}) %collective-permute-start) | collective-permute-done | bytes 131104 | tf_op jit(solution)/shard_map/ppermute | solution.py:22
  10.6 0.1 turn_pair.1.refs_1_
  10.8 2.5 %collective-permute-start.2 = (bf16[1,128,4096]{2,1,0:T(8,128)(2,1)}, bf16[1,128,4096]{2,1,0:T(8,128)(2,1)S(1)}, u32[]{:S(2)}, u32[]{:S(2)}) collective-permute-start(bf16[1,128,4096]{2,1,0:T(8,128)(2,1)} %param.7), channel_id=1, source_target_pairs={{480,0},{0,32},{32,64},{64,96},{96,128},{128,160},{160,192},{192,2... | collective-permute-start | bytes 3145736 | tf_op jit(solution)/shard_map/ppermute | solution.py:22
  13.2 9.7 %collective-permute-start.3 = (bf16[256,512]{1,0:T(8,128)(2,1)S(1)}, bf16[256,512]{1,0:T(8,128)(2,1)S(1)}, u32[]{:S(2)}, u32[]{:S(2)}) collective-permute-start(bf16[256,512]{1,0:T(8,128)(2,1)S(1)} %turn_pair.1.refs_1_), channel_id=1, source_target_pairs={{8,0},{28,4},{16,8},{4,12},{24,16},{12,20},{0,24},{20,28},{9,1},{2... | collective-permute-start | bytes 786440 | tf_op jit(solution)/shard_map/ppermute | solution.py:240
  23.0 1.9 %collective-permute-start.5 = (bf16[256,512]{1,0:T(8,128)(2,1)S(1)}, bf16[256,512]{1,0:T(8,128)(2,1)S(1)}, u32[]{:S(2)}, u32[]{:S(2)}) collective-permute-start(bf16[256,512]{1,0:T(8,128)(2,1)S(1)} %turn_pair.1.refs_1_), channel_id=1, source_target_pairs={{28,0},{8,4},{4,8},{16,12},{12,16},{24,20},{20,24},{0,28},{29,1},{... | collective-permute-start | bytes 786440 | tf_op jit(solution)/shard_map/ppermute | solution.py:241
  24.9 3.8 %collective-permute-done.3.refs_2_ = bf16[256,512]{1,0:T(8,128)(2,1)S(1)} collective-permute-done((bf16[256,512]{1,0:T(8,128)(2,1)S(1)}, bf16[256,512]{1,0:T(8,128)(2,1)S(1)}, u32[]{:S(2)}, u32[]{:S(2)}) %collective-permute-start.3) | collective-permute-done | bytes 262176 | tf_op jit(solution)/shard_map/ppermute | solution.py:240
  28.7 4.1 %collective-permute-start.4 = (bf16[256,512]{1,0:T(8,128)(2,1)S(1)}, bf16[256,512]{1,0:T(8,128)(2,1)S(1)}, u32[]{:S(2)}, u32[]{:S(2)}) collective-permute-start(bf16[256,512]{1,0:T(8,128)(2,1)S(1)} %collective-permute-done.3.refs_2_), channel_id=1, source_target_pairs={{28,0},{8,4},{4,8},{16,12},{12,16},{24,20},{20,24},{0,28},{29,1},{... | collective-permute-start | bytes 786440 | tf_op jit(solution)/shard_map/ppermute | solution.py:242
  32.8 0.2 select_convert_fusion.2
  33.0 0.0 collective-permute-done.2
  33.0 0.5 %turn.1.refs_0_ = bf16[4096,128]{1,0:T(8,128)(2,1)S(1)} custom-call(bf16[128,4096]{1,0:T(8,128)(2,1)S(1)} %bitcast.21, f32[256,128]{1,0:T(8,128)S(1)} %get-tuple-element.22.cosine_ref, f32[256,128]{1,0:T(8,128)S(1)} %get-tuple-element.21.sine_ref), custom_call_target="tpu_custom_call" | custom-call | tf_op jit(solution)/shard_map/turn/pallas_call | solution.py:93
  33.6 0.8 %collective-permute-done.5.refs_3_ = bf16[256,512]{1,0:T(8,128)(2,1)S(1)} collective-permute-done((bf16[256,512]{1,0:T(8,128)(2,1)S(1)}, bf16[256,512]{1,0:T(8,128)(2,1)S(1)}, u32[]{:S(2)}, u32[]{:S(2)}) %collective-permute-start.5) | collective-permute-done | bytes 262176 | tf_op jit(solution)/shard_map/ppermute | solution.py:241
  34.3 4.0 %attend.2 = (f32[4096,256]{1,0:T(8,128)S(1)}, f32[4096,128]{1,0:T(8,128)S(1)}) custom-call(bf16[4096,128]{1,0:T(8,128)(2,1)S(1)} %turn.1.refs_0_, bf16[256,512]{1,0:T(8,128)(2,1)S(1)} %turn_pair.1.refs_1_, bf16[256,512]{1,0:T(8,128)(2,1)S(1)} %collective-permute-done.3.refs_2_, bf16[256,512]{1,0:T(8,128)(2,1)S(1)} %collective-permute-done.5.refs_3_, ...), custom_call_target="tpu_custom_call" | custom-call | flops 1000 | bytes 1000 | tf_op jit(solution)/shard_map/attend/pallas_call | solution.py:192
  38.4 1.6 %collective-permute-done.4.refs_1_ = bf16[256,512]{1,0:T(8,128)(2,1)S(1)} collective-permute-done((bf16[256,512]{1,0:T(8,128)(2,1)S(1)}, bf16[256,512]{1,0:T(8,128)(2,1)S(1)}, u32[]{:S(2)}, u32[]{:S(2)}) %collective-permute-start.4) | collective-permute-done | bytes 262176 | tf_op jit(solution)/shard_map/ppermute | solution.py:242
  39.9 3.7 %attend.3 = bf16[128,4096]{1,0:T(8,128)(2,1)} custom-call(bf16[4096,128]{1,0:T(8,128)(2,1)S(1)} %turn.1.refs_0_, bf16[256,512]{1,0:T(8,128)(2,1)S(1)} %collective-permute-done.4.refs_1_, bf16[256,128]{1,0:T(8,128)(2,1)S(1)} %get-tuple-element.29.refs_2_, f32[4096,256]{1,0:T(8,128)S(1)} %get-tuple-element.11.refs_3_, f32[4096,128]{1,0:T(8,128)S(1)} %get-tuple-element.12.refs_4_), custom_call_target="tpu_custom_call" | custom-call | flops 1000 | bytes 1000 | tf_op jit(solution)/shard_map/attend/pallas_call | solution.py:192
  (3 shorter events, 0.0 us)
Async XLA Ops:
  0.9 8.8 %collective-permute-start.1 = (bf16[128,512]{1,0:T(8,128)(2,1)S(1)}, bf16[128,512]{1,0:T(8,128)(2,1)S(1)}, u32[]{:S(2)}, u32[]{:S(2)}) collective-permute-start(bf16[128,512]{1,0:T(8,128)(2,1)S(1)} %pad_maximum_fusion.1), channel_id=1, source_target_pairs={{484,0},{480,4},{492,8},{488,12},{500,16},{496,20},{508,24},{504,2... | collective-permute-start | bytes 393224 | tf_op jit(solution)/shard_map/ppermute | solution.py:209
  7.3 3.3 %collective-permute-start = (bf16[128,512]{1,0:T(8,128)(2,1)S(1)}, bf16[128,512]{1,0:T(8,128)(2,1)S(1)}, u32[]{:S(2)}, u32[]{:S(2)}) collective-permute-start(bf16[128,512]{1,0:T(8,128)(2,1)S(1)} %pad_maximum_fusion.1), channel_id=1, source_target_pairs={{480,0},{0,32},{32,64},{64,96},{96,128},{128,160},{160,192},{192,2... | collective-permute-start | bytes 393224 | tf_op jit(solution)/shard_map/ppermute | solution.py:22
  10.8 22.3 %collective-permute-start.2 = (bf16[1,128,4096]{2,1,0:T(8,128)(2,1)}, bf16[1,128,4096]{2,1,0:T(8,128)(2,1)S(1)}, u32[]{:S(2)}, u32[]{:S(2)}) collective-permute-start(bf16[1,128,4096]{2,1,0:T(8,128)(2,1)} %param.7), channel_id=1, source_target_pairs={{480,0},{0,32},{32,64},{64,96},{96,128},{128,160},{160,192},{192,2... | collective-permute-start | bytes 3145736 | tf_op jit(solution)/shard_map/ppermute | solution.py:22
  13.2 15.5 %collective-permute-start.3 = (bf16[256,512]{1,0:T(8,128)(2,1)S(1)}, bf16[256,512]{1,0:T(8,128)(2,1)S(1)}, u32[]{:S(2)}, u32[]{:S(2)}) collective-permute-start(bf16[256,512]{1,0:T(8,128)(2,1)S(1)} %turn_pair.1.refs_1_), channel_id=1, source_target_pairs={{8,0},{28,4},{16,8},{4,12},{24,16},{12,20},{0,24},{20,28},{9,1},{2... | collective-permute-start | bytes 786440 | tf_op jit(solution)/shard_map/ppermute | solution.py:240
  23.0 11.3 %collective-permute-start.5 = (bf16[256,512]{1,0:T(8,128)(2,1)S(1)}, bf16[256,512]{1,0:T(8,128)(2,1)S(1)}, u32[]{:S(2)}, u32[]{:S(2)}) collective-permute-start(bf16[256,512]{1,0:T(8,128)(2,1)S(1)} %turn_pair.1.refs_1_), channel_id=1, source_target_pairs={{28,0},{8,4},{4,8},{16,12},{12,16},{24,20},{20,24},{0,28},{29,1},{... | collective-permute-start | bytes 786440 | tf_op jit(solution)/shard_map/ppermute | solution.py:241
  28.7 11.2 %collective-permute-start.4 = (bf16[256,512]{1,0:T(8,128)(2,1)S(1)}, bf16[256,512]{1,0:T(8,128)(2,1)S(1)}, u32[]{:S(2)}, u32[]{:S(2)}) collective-permute-start(bf16[256,512]{1,0:T(8,128)(2,1)S(1)} %collective-permute-done.3.refs_2_), channel_id=1, source_target_pairs={{28,0},{8,4},{4,8},{16,12},{12,16},{24,20},{20,24},{0,28},{29,1},{... | collective-permute-start | bytes 786440 | tf_op jit(solution)/shard_map/ppermute | solution.py:242

commit v4 on v3

--- a/solution.py
+++ b/solution.py
@@ -13,7 +13,7 @@
 MASKED = -1e30
 SCALE = math.log2(math.e) / math.sqrt(HEAD_DIM)
 HEADS_PER_PASS = 4
-GROUPS = ((0, 1, 2), (3,))
+GROUPS = ((0,), (1, 2), (3,))
 
 
 def shifted(block, axis, distance):
@@ -141,19 +141,26 @@
             scores = following
             if step + 1 < (key_head + 1) * steps:
                 following = score(keys, step + 1)
-            highest = jnp.max(scores, axis=-1, keepdims=True)
+            highest = jnp.broadcast_to(jnp.max(scores, axis=-1, keepdims=True), (size, HEAD_DIM))
             if not first:
-                before = before_highest_ref[place][:, :1]
+                before = before_highest_ref[place]
                 highest = jnp.maximum(highest, before)
-            weights = jnp.exp2((scores - highest) * SCALE).astype(jnp.bfloat16)
+            weights = jnp.concatenate(
+                [
+                    jnp.exp2((scores[:, i : i + HEAD_DIM] - highest) * SCALE).astype(jnp.bfloat16)
+                    for i in range(0, tokens, HEAD_DIM)
+                ],
+                axis=1,
+            )
             summed = lax.dot_general(
                 weights, values, (((1,), (0,)), ((), ())), preferred_element_type=jnp.float32
             )
             if not first:
-                summed = summed + before_ref[place] * jnp.exp2((before - highest) * SCALE)
+                factor = jnp.exp2((before - highest) * SCALE)
+                summed = summed + before_ref[place] * jnp.concatenate([factor, factor], axis=1)
             if not last:
                 sums_ref[place] = summed
-                highest_ref[place] = jnp.broadcast_to(highest, (size, HEAD_DIM))
+                highest_ref[place] = highest
                 continue
             attended = (summed[:, :HEAD_DIM] / summed[:, HEAD_DIM:]).astype(jnp.bfloat16)
             for i in range(HEADS_PER_PASS):
@@ -234,9 +241,9 @@
         jnp.where(jnp.concatenate(pos)[:, None] <= own_pos[None, :], 0.0, MASKED).astype(jnp.bfloat16)
         for pos in key_pos
     ]
+    query_rows, own_rows = lax.optimization_barrier((query_rows, own_rows))
+    query_in = shifted(query_rows, "section", 1)
     pair_rows = turn_pair(own_rows, partner_rows, cosine, sine)
-    query_rows, pair_rows = lax.optimization_barrier((query_rows, pair_rows))
-    query_in = shifted(query_rows, "section", 1)
     second = lax.ppermute(pair_rows, "ctx", route(2))
     beside_rows = lax.ppermute(pair_rows, "ctx", route(-1))
     across = lax.ppermute(second, "ctx", route(-1))

time: 44.4 us -> 42.3 us (0.953); the launches traced: 43.6 us -> 42 us
  waiting for transfers between devices: 7.04 us -> 6.16 us
  Pallas kernels: 8.32 us -> 7.68 us
    ppermute x1, starting transfers between devices: 6.4 us -> 3.73 us  [per_device(): lax.ppermute(rows, ('section', 'ctx'), [((s - 1) % sections * owners + (c...]
    ppermute x1, starting transfers between devices: 4.08 us -> 5.18 us  [per_device(): across = lax.ppermute(second, 'ctx', route(-1))]
    ppermute x2, starting transfers between devices: 2.51 us -> 3.36 us  [shifted(): return lax.ppermute(block, axis, route)]
    ppermute x1, waiting for transfers between devices: 0.78 us -> 0.01 us  [per_device(): beside_rows = lax.ppermute(pair_rows, 'ctx', route(-1))]
    pallas_call x2 -> x3, Pallas kernels: 7.71 us -> 7.06 us  [attend(): pl.pallas_call(partial(attend_kernel, pieces=len(pieces), first=not carri...]
    ppermute x1, starting transfers between devices: 9.75 us -> 10.4 us  [per_device(): second = lax.ppermute(pair_rows, 'ctx', route(2))]
    ppermute x1, waiting for transfers between devices: 1.58 us -> 1.06 us  [per_device(): across = lax.ppermute(second, 'ctx', route(-1))]
  transfers between devices with their start and end apart: 6 -> 6, of which waited for: 4 -> 3; matrix products, arithmetic and copies ran while one was open for 6% -> 6% of each run, Pallas kernels for 10% -> 12%
where the time goes in v4:
time: 42.3 us; the launch traced here: 42 us
  starting transfers between devices  24.6 us (58%)
  Pallas kernels  7.68 us (18%)
  waiting for transfers between devices  6.16 us (15%)
  other arithmetic  2.38 us (6%)
  local copies, waits for them, and re-layouts  0.98 us (2%)
    ppermute x1, starting transfers between devices, per_device(): second = lax.ppermute(pair_rows, 'ctx', route(2))  10.4 us
    pallas_call x3, Pallas kernels, attend(): pl.pallas_call(partial(attend_kernel, pieces=len(pieces), first=not carri...  7.06 us
    ppermute x1, starting transfers between devices, per_device(): across = lax.ppermute(second, 'ctx', route(-1))  5.18 us
    ppermute x1, waiting for transfers between devices, per_device(): second = lax.ppermute(pair_rows, 'ctx', route(2))  3.91 us
    ppermute x1, starting transfers between devices, per_device(): lax.ppermute(rows, ('section', 'ctx'), [((s - 1) % sections * owners + (c...  3.73 us
    ppermute x2, starting transfers between devices, shifted(): return lax.ppermute(block, axis, route)  3.36 us
    ppermute x1, starting transfers between devices, per_device(): beside_rows = lax.ppermute(pair_rows, 'ctx', route(-1))  1.98 us
    mul x1, other arithmetic, turn_tables(): return (jnp.cos(angles), jnp.sin(angles) * sign[None, :])  1.26 us
  transfers between devices with their start and end apart: 6, of which 3 were waited for; matrix products, arithmetic and copies ran while one was open for 6% of the time, Pallas kernels for 12%

profile of v4, /device:TPU:1, one launch (start us, length us, event | category | flops | bytes accessed | tf_op | source)
XLA Modules:
  0.0 42.0 jit_solution(8190907823499892210)
XLA Ops:
  0.0 0.9 %pad_maximum_fusion = bf16[128,512]{1,0:T(8,128)(2,1)S(1)} fusion(bf16[128,256]{1,0:T(8,128)(2,1)} %bitcast.22, bf16[128,256]{1,0:T(8,128)(2,1)} %bitcast.23), kind=kLoop, calls=%fused_computation | loop fusion | flops 262144 | bytes 262144 | tf_op jit(solution)/shard_map/concatenate | solution.py:214
  0.9 2.7 %collective-permute-start = (bf16[128,512]{1,0:T(8,128)(2,1)S(1)}, bf16[128,512]{1,0:T(8,128)(2,1)S(1)}, u32[]{:S(2)}, u32[]{:S(2)}) collective-permute-start(bf16[128,512]{1,0:T(8,128)(2,1)S(1)} %pad_maximum_fusion), channel_id=1, source_target_pairs={{480,0},{0,32},{32,64},{64,96},{96,128},{128,160},{160,192},{192,2... | collective-permute-start | bytes 393224 | tf_op jit(solution)/shard_map/ppermute | solution.py:22
  3.6 3.7 %collective-permute-start.2 = (bf16[128,512]{1,0:T(8,128)(2,1)S(1)}, bf16[128,512]{1,0:T(8,128)(2,1)S(1)}, u32[]{:S(2)}, u32[]{:S(2)}) collective-permute-start(bf16[128,512]{1,0:T(8,128)(2,1)S(1)} %pad_maximum_fusion), channel_id=1, source_target_pairs={{484,0},{480,4},{492,8},{488,12},{500,16},{496,20},{508,24},{504,2... | collective-permute-start | bytes 393224 | tf_op jit(solution)/shard_map/ppermute | solution.py:216
  7.4 1.2 %collective-permute-done.own_ref = bf16[128,512]{1,0:T(8,128)(2,1)S(1)} collective-permute-done((bf16[128,512]{1,0:T(8,128)(2,1)S(1)}, bf16[128,512]{1,0:T(8,128)(2,1)S(1)}, u32[]{:S(2)}, u32[]{:S(2)}) %collective-permute-start) | collective-permute-done | bytes 131104 | tf_op jit(solution)/shard_map/ppermute | solution.py:22
  8.6 0.7 %collective-permute-start.1 = (bf16[1,128,4096]{2,1,0:T(8,128)(2,1)}, bf16[1,128,4096]{2,1,0:T(8,128)(2,1)S(1)}, u32[]{:S(2)}, u32[]{:S(2)}) collective-permute-start(bf16[1,128,4096]{2,1,0:T(8,128)(2,1)} %param.7), channel_id=1, source_target_pairs={{480,0},{0,32},{32,64},{64,96},{96,128},{128,160},{160,192},{192,2... | collective-permute-start | bytes 3145736 | tf_op jit(solution)/shard_map/ppermute | solution.py:22
  9.3 1.0 %fusion.7 = (s32[128]{0:T(128)S(1)}, s32[128]{0:T(128)S(1)}, s32[128]{0:T(128)S(1)}, s32[128]{0:T(128)S(1)}, s32[128]{0:T(128)S(1)}, /*index=5*/s32[128]{0:T(128)S(1)}, s32[128]{0:T(128)S(1)}, s32[128]{0:T(128)S(1)}) fusion(s32[8,128]{1,0:T(8,128)} %bitcast.24, s32[]{:T(128)S(6)} %select_n.95, s32[]{:T(128)S(6)} %select_n.100, s32[]{:T(128)S(6)} %select_n.99, ...), kind=kLoop, calls=%fused_computation.32 | loop fusion | bytes 8224 | tf_op jit(solution)/shard_map/jit(dynamic_index_in_dim)/squeeze | solution.py:229
  10.3 1.3 %sine_multiply_fusion = (f32[256,128]{1,0:T(8,128)S(1)}, f32[256,128]{1,0:T(8,128)S(1)}) fusion(f32[128]{0:T(128)} %constant.105.clone, f32[128]{0:T(128)} %constant.103.clone, f32[256]{0:T(256)S(1)} %get-tuple-element.29, f32[128]{0:T(128)} %constant.104.clone, f32[256]{0:T(256)S(1)} %get-tuple-element.28), kind=kLoop, calls=%fused_computation.6 | loop fusion | flops 131072 | bytes 265728 | tf_op jit(solution)/shard_map/mul | solution.py:44
  11.6 0.0 collective-permute-done.2.partner_ref
  11.6 0.1 turn_pair.1.refs_1_
  11.7 10.4 %collective-permute-start.3 = (bf16[256,512]{1,0:T(8,128)(2,1)S(1)}, bf16[256,512]{1,0:T(8,128)(2,1)S(1)}, u32[]{:S(2)}, u32[]{:S(2)}) collective-permute-start(bf16[256,512]{1,0:T(8,128)(2,1)S(1)} %turn_pair.1.refs_1_), channel_id=1, source_target_pairs={{8,0},{28,4},{16,8},{4,12},{24,16},{12,20},{0,24},{20,28},{9,1},{2... | collective-permute-start | bytes 786440 | tf_op jit(solution)/shard_map/ppermute | solution.py:247
  22.1 2.0 %collective-permute-start.5 = (bf16[256,512]{1,0:T(8,128)(2,1)S(1)}, bf16[256,512]{1,0:T(8,128)(2,1)S(1)}, u32[]{:S(2)}, u32[]{:S(2)}) collective-permute-start(bf16[256,512]{1,0:T(8,128)(2,1)S(1)} %turn_pair.1.refs_1_), channel_id=1, source_target_pairs={{28,0},{8,4},{4,8},{16,12},{12,16},{24,20},{20,24},{0,28},{29,1},{... | collective-permute-start | bytes 786440 | tf_op jit(solution)/shard_map/ppermute | solution.py:248
  24.1 3.9 %collective-permute-done.3.refs_1_ = bf16[256,512]{1,0:T(8,128)(2,1)S(1)} collective-permute-done((bf16[256,512]{1,0:T(8,128)(2,1)S(1)}, bf16[256,512]{1,0:T(8,128)(2,1)S(1)}, u32[]{:S(2)}, u32[]{:S(2)}) %collective-permute-start.3) | collective-permute-done | bytes 262176 | tf_op jit(solution)/shard_map/ppermute | solution.py:247
  28.0 5.2 %collective-permute-start.4 = (bf16[256,512]{1,0:T(8,128)(2,1)S(1)}, bf16[256,512]{1,0:T(8,128)(2,1)S(1)}, u32[]{:S(2)}, u32[]{:S(2)}) collective-permute-start(bf16[256,512]{1,0:T(8,128)(2,1)S(1)} %collective-permute-done.3.refs_1_), channel_id=1, source_target_pairs={{28,0},{8,4},{4,8},{16,12},{12,16},{24,20},{20,24},{0,28},{29,1},{... | collective-permute-start | bytes 786440 | tf_op jit(solution)/shard_map/ppermute | solution.py:249
  33.2 0.2 select_convert_fusion
  33.4 0.0 collective-permute-done.1
  33.4 0.5 %turn.1.refs_0_ = bf16[4096,128]{1,0:T(8,128)(2,1)S(1)} custom-call(bf16[128,4096]{1,0:T(8,128)(2,1)S(1)} %bitcast.21, f32[256,128]{1,0:T(8,128)S(1)} %get-tuple-element.26.cosine_ref, f32[256,128]{1,0:T(8,128)S(1)} %get-tuple-element.25.sine_ref), custom_call_target="tpu_custom_call" | custom-call | tf_op jit(solution)/shard_map/turn/pallas_call | solution.py:93
  33.9 1.5 %attend.3 = (f32[4096,256]{1,0:T(8,128)S(1)}, f32[4096,128]{1,0:T(8,128)S(1)}) custom-call(bf16[4096,128]{1,0:T(8,128)(2,1)S(1)} %turn.1.refs_0_, bf16[256,512]{1,0:T(8,128)(2,1)S(1)} %turn_pair.1.refs_1_, bf16[256,128]{1,0:T(8,128)(2,1)S(1)} %get-tuple-element.30.refs_2_), custom_call_target="tpu_custom_call" | custom-call | flops 1000 | bytes 1000 | tf_op jit(solution)/shard_map/attend/pallas_call | solution.py:199
  35.4 0.0 collective-permute-done.5.refs_2_
  35.4 2.9 %attend.4 = (f32[4096,256]{1,0:T(8,128)S(1)}, f32[4096,128]{1,0:T(8,128)S(1)}) custom-call(bf16[4096,128]{1,0:T(8,128)(2,1)S(1)} %turn.1.refs_0_, bf16[256,512]{1,0:T(8,128)(2,1)S(1)} %collective-permute-done.3.refs_1_, bf16[256,512]{1,0:T(8,128)(2,1)S(1)} %collective-permute-done.5.refs_2_, bf16[512,128]{1,0:T(8,128)(2,1)S(1)} %pad_maximum_fusion.1.refs_3_, ...), custom_call_target="tpu_custom_call" | custom-call | flops 1000 | bytes 1000 | tf_op jit(solution)/shard_map/attend/pallas_call | solution.py:199
  38.3 1.1 %collective-permute-done.4.refs_1_ = bf16[256,512]{1,0:T(8,128)(2,1)S(1)} collective-permute-done((bf16[256,512]{1,0:T(8,128)(2,1)S(1)}, bf16[256,512]{1,0:T(8,128)(2,1)S(1)}, u32[]{:S(2)}, u32[]{:S(2)}) %collective-permute-start.4) | collective-permute-done | bytes 262176 | tf_op jit(solution)/shard_map/ppermute | solution.py:249
  39.3 2.7 %attend.5 = bf16[128,4096]{1,0:T(8,128)(2,1)} custom-call(bf16[4096,128]{1,0:T(8,128)(2,1)S(1)} %turn.1.refs_0_, bf16[256,512]{1,0:T(8,128)(2,1)S(1)} %collective-permute-done.4.refs_1_, bf16[256,128]{1,0:T(8,128)(2,1)S(1)} %get-tuple-element.33.refs_2_, f32[4096,256]{1,0:T(8,128)S(1)} %get-tuple-element.15.refs_3_, f32[4096,128]{1,0:T(8,128)S(1)} %get-tuple-element.16.refs_4_), custom_call_target="tpu_custom_call" | custom-call | flops 1000 | bytes 1000 | tf_op jit(solution)/shard_map/attend/pallas_call | solution.py:199
  (3 shorter events, 0.0 us)
Async XLA Ops:
  0.9 7.7 %collective-permute-start = (bf16[128,512]{1,0:T(8,128)(2,1)S(1)}, bf16[128,512]{1,0:T(8,128)(2,1)S(1)}, u32[]{:S(2)}, u32[]{:S(2)}) collective-permute-start(bf16[128,512]{1,0:T(8,128)(2,1)S(1)} %pad_maximum_fusion), channel_id=1, source_target_pairs={{480,0},{0,32},{32,64},{64,96},{96,128},{128,160},{160,192},{192,2... | collective-permute-start | bytes 393224 | tf_op jit(solution)/shard_map/ppermute | solution.py:22
  3.6 8.0 %collective-permute-start.2 = (bf16[128,512]{1,0:T(8,128)(2,1)S(1)}, bf16[128,512]{1,0:T(8,128)(2,1)S(1)}, u32[]{:S(2)}, u32[]{:S(2)}) collective-permute-start(bf16[128,512]{1,0:T(8,128)(2,1)S(1)} %pad_maximum_fusion), channel_id=1, source_target_pairs={{484,0},{480,4},{492,8},{488,12},{500,16},{496,20},{508,24},{504,2... | collective-permute-start | bytes 393224 | tf_op jit(solution)/shard_map/ppermute | solution.py:216
  8.6 24.8 %collective-permute-start.1 = (bf16[1,128,4096]{2,1,0:T(8,128)(2,1)}, bf16[1,128,4096]{2,1,0:T(8,128)(2,1)S(1)}, u32[]{:S(2)}, u32[]{:S(2)}) collective-permute-start(bf16[1,128,4096]{2,1,0:T(8,128)(2,1)} %param.7), channel_id=1, source_target_pairs={{480,0},{0,32},{32,64},{64,96},{96,128},{128,160},{160,192},{192,2... | collective-permute-start | bytes 3145736 | tf_op jit(solution)/shard_map/ppermute | solution.py:22
  11.7 16.3 %collective-permute-start.3 = (bf16[256,512]{1,0:T(8,128)(2,1)S(1)}, bf16[256,512]{1,0:T(8,128)(2,1)S(1)}, u32[]{:S(2)}, u32[]{:S(2)}) collective-permute-start(bf16[256,512]{1,0:T(8,128)(2,1)S(1)} %turn_pair.1.refs_1_), channel_id=1, source_target_pairs={{8,0},{28,4},{16,8},{4,12},{24,16},{12,20},{0,24},{20,28},{9,1},{2... | collective-permute-start | bytes 786440 | tf_op jit(solution)/shard_map/ppermute | solution.py:247
  22.1 13.3 %collective-permute-start.5 = (bf16[256,512]{1,0:T(8,128)(2,1)S(1)}, bf16[256,512]{1,0:T(8,128)(2,1)S(1)}, u32[]{:S(2)}, u32[]{:S(2)}) collective-permute-start(bf16[256,512]{1,0:T(8,128)(2,1)S(1)} %turn_pair.1.refs_1_), channel_id=1, source_target_pairs={{28,0},{8,4},{4,8},{16,12},{12,16},{24,20},{20,24},{0,28},{29,1},{... | collective-permute-start | bytes 786440 | tf_op jit(solution)/shard_map/ppermute | solution.py:248
  28.0 11.4 %collective-permute-start.4 = (bf16[256,512]{1,0:T(8,128)(2,1)S(1)}, bf16[256,512]{1,0:T(8,128)(2,1)S(1)}, u32[]{:S(2)}, u32[]{:S(2)}) collective-permute-start(bf16[256,512]{1,0:T(8,128)(2,1)S(1)} %collective-permute-done.3.refs_1_), channel_id=1, source_target_pairs={{28,0},{8,4},{4,8},{16,12},{12,16},{24,20},{20,24},{0,28},{29,1},{... | collective-permute-start | bytes 786440 | tf_op jit(solution)/shard_map/ppermute | solution.py:249

commit v5 on v4

--- a/solution.py
+++ b/solution.py
@@ -13,7 +13,7 @@
 MASKED = -1e30
 SCALE = math.log2(math.e) / math.sqrt(HEAD_DIM)
 HEADS_PER_PASS = 4
-GROUPS = ((0,), (1, 2), (3,))
+GROUPS = ((0, 1, 2), (3,))
 
 
 def shifted(block, axis, distance):
@@ -132,15 +132,15 @@
         )
 
     copies = []
+    keys = [jnp.concatenate([part(i), mask], axis=1) for i in range(key_heads)]
+    following = score(keys[0], 0)
     for key_head in range(key_heads):
-        keys = jnp.concatenate([part(key_head), mask], axis=1)
         values = jnp.concatenate([part(key_heads + key_head), ones], axis=1)
-        following = score(keys, key_head * steps)
         for step in range(key_head * steps, (key_head + 1) * steps):
             place = pl.ds(step * size, size)
             scores = following
-            if step + 1 < (key_head + 1) * steps:
-                following = score(keys, step + 1)
+            if step + 1 < key_heads * steps:
+                following = score(keys[(step + 1) // steps], step + 1)
             highest = jnp.broadcast_to(jnp.max(scores, axis=-1, keepdims=True), (size, HEAD_DIM))
             if not first:
                 before = before_highest_ref[place]
@@ -163,11 +163,10 @@
                 highest_ref[place] = highest
                 continue
             attended = (summed[:, :HEAD_DIM] / summed[:, HEAD_DIM:]).astype(jnp.bfloat16)
-            for i in range(HEADS_PER_PASS):
-                head = step * HEADS_PER_PASS + i
-                held_ref[:, head * HEAD_DIM : (head + 1) * HEAD_DIM] = attended[
-                    i * rows : (i + 1) * rows
-                ]
+            first_column = step * HEADS_PER_PASS * HEAD_DIM
+            held_ref[:, first_column : first_column + HEADS_PER_PASS * HEAD_DIM] = jnp.concatenate(
+                [attended[i * rows : (i + 1) * rows] for i in range(HEADS_PER_PASS)], axis=1
+            )
             columns = pl.ds(step * HEADS_PER_PASS * HEAD_DIM, HEADS_PER_PASS * HEAD_DIM)
             copies.append(
                 pltpu.make_async_copy(held_ref.at[:, columns], out_ref.at[:, columns], sent.at[step])

time: 42.3 us -> 42.2 us (level)
  Pallas kernels: 7.68 us -> 7.02 us
  waiting for transfers between devices: 6.16 us -> 6.72 us
    pallas_call x3 -> x2, Pallas kernels: 7.06 us -> 6.4 us  [attend(): pl.pallas_call(partial(attend_kernel, pieces=len(pieces), first=not carri...]
  transfers between devices with their start and end apart: 6 -> 6, of which waited for: 3 -> 4; matrix products, arithmetic and copies ran while one was open for 6% -> 6% of each run, Pallas kernels for 12% -> 11%
where the time goes in v5:
time: 42.2 us; the launch traced here: 41.9 us
  starting transfers between devices  24.6 us (58%)
  Pallas kernels  7.02 us (17%)
  waiting for transfers between devices  6.72 us (16%)
  other arithmetic  2.39 us (6%)
  local copies, waits for them, and re-layouts  0.98 us (2%)
    ppermute x1, starting transfers between devices, per_device(): second = lax.ppermute(pair_rows, 'ctx', route(2))  10.4 us
    pallas_call x2, Pallas kernels, attend(): pl.pallas_call(partial(attend_kernel, pieces=len(pieces), first=not carri...  6.4 us
    ppermute x1, starting transfers between devices, per_device(): across = lax.ppermute(second, 'ctx', route(-1))  5.18 us
    ppermute x1, waiting for transfers between devices, per_device(): second = lax.ppermute(pair_rows, 'ctx', route(2))  3.91 us
    ppermute x1, starting transfers between devices, per_device(): lax.ppermute(rows, ('section', 'ctx'), [((s - 1) % sections * owners + (c...  3.73 us
    ppermute x2, starting transfers between devices, shifted(): return lax.ppermute(block, axis, route)  3.36 us
    ppermute x1, starting transfers between devices, per_device(): beside_rows = lax.ppermute(pair_rows, 'ctx', route(-1))  1.98 us
    ppermute x1, waiting for transfers between devices, per_device(): across = lax.ppermute(second, 'ctx', route(-1))  1.37 us
  transfers between devices with their start and end apart: 6, of which 4 were waited for; matrix products, arithmetic and copies ran while one was open for 6% of the time, Pallas kernels for 11%

profile of v5, /device:TPU:1, one launch (start us, length us, event | category | flops | bytes accessed | tf_op | source)
XLA Modules:
  0.0 41.9 jit_solution(16712076529749158755)
XLA Ops:
  0.0 0.9 %pad_maximum_fusion.1 = bf16[128,512]{1,0:T(8,128)(2,1)S(1)} fusion(bf16[128,256]{1,0:T(8,128)(2,1)} %bitcast.22, bf16[128,256]{1,0:T(8,128)(2,1)} %bitcast.23), kind=kLoop, calls=%fused_computation.1 | loop fusion | flops 262144 | bytes 262144 | tf_op jit(solution)/shard_map/concatenate | solution.py:213
  0.9 2.7 %collective-permute-start = (bf16[128,512]{1,0:T(8,128)(2,1)S(1)}, bf16[128,512]{1,0:T(8,128)(2,1)S(1)}, u32[]{:S(2)}, u32[]{:S(2)}) collective-permute-start(bf16[128,512]{1,0:T(8,128)(2,1)S(1)} %pad_maximum_fusion.1), channel_id=1, source_target_pairs={{480,0},{0,32},{32,64},{64,96},{96,128},{128,160},{160,192},{192,2... | collective-permute-start | bytes 393224 | tf_op jit(solution)/shard_map/ppermute | solution.py:22
  3.6 3.7 %collective-permute-start.2 = (bf16[128,512]{1,0:T(8,128)(2,1)S(1)}, bf16[128,512]{1,0:T(8,128)(2,1)S(1)}, u32[]{:S(2)}, u32[]{:S(2)}) collective-permute-start(bf16[128,512]{1,0:T(8,128)(2,1)S(1)} %pad_maximum_fusion.1), channel_id=1, source_target_pairs={{484,0},{480,4},{492,8},{488,12},{500,16},{496,20},{508,24},{504,2... | collective-permute-start | bytes 393224 | tf_op jit(solution)/shard_map/ppermute | solution.py:215
  7.4 1.2 %collective-permute-done.own_ref = bf16[128,512]{1,0:T(8,128)(2,1)S(1)} collective-permute-done((bf16[128,512]{1,0:T(8,128)(2,1)S(1)}, bf16[128,512]{1,0:T(8,128)(2,1)S(1)}, u32[]{:S(2)}, u32[]{:S(2)}) %collective-permute-start) | collective-permute-done | bytes 131104 | tf_op jit(solution)/shard_map/ppermute | solution.py:22
  8.6 0.7 %collective-permute-start.1 = (bf16[1,128,4096]{2,1,0:T(8,128)(2,1)}, bf16[1,128,4096]{2,1,0:T(8,128)(2,1)S(1)}, u32[]{:S(2)}, u32[]{:S(2)}) collective-permute-start(bf16[1,128,4096]{2,1,0:T(8,128)(2,1)} %param.7), channel_id=1, source_target_pairs={{480,0},{0,32},{32,64},{64,96},{96,128},{128,160},{160,192},{192,2... | collective-permute-start | bytes 3145736 | tf_op jit(solution)/shard_map/ppermute | solution.py:22
  9.3 1.0 %fusion.7 = (s32[128]{0:T(128)S(1)}, s32[128]{0:T(128)S(1)}, s32[128]{0:T(128)S(1)}, s32[128]{0:T(128)S(1)}, s32[128]{0:T(128)S(1)}, /*index=5*/s32[128]{0:T(128)S(1)}, s32[128]{0:T(128)S(1)}, s32[128]{0:T(128)S(1)}) fusion(s32[8,128]{1,0:T(8,128)} %bitcast.24, s32[]{:T(128)S(6)} %select_n.96, s32[]{:T(128)S(6)} %select_n.101, s32[]{:T(128)S(6)} %select_n.100, ...), kind=kLoop, calls=%fused_computation.32 | loop fusion | bytes 8224 | tf_op jit(solution)/shard_map/jit(dynamic_index_in_dim)/squeeze | solution.py:228
  10.3 1.3 %sine_multiply_fusion = (f32[256,128]{1,0:T(8,128)S(1)}, f32[256,128]{1,0:T(8,128)S(1)}) fusion(f32[128]{0:T(128)} %constant.105.clone, f32[128]{0:T(128)} %constant.103.clone, f32[256]{0:T(256)S(1)} %get-tuple-element.25, f32[128]{0:T(128)} %constant.104.clone, f32[256]{0:T(256)S(1)} %get-tuple-element.24), kind=kLoop, calls=%fused_computation.6 | loop fusion | flops 131072 | bytes 265728 | tf_op jit(solution)/shard_map/mul | solution.py:44
  11.6 0.0 collective-permute-done.2.partner_ref
  11.6 0.1 turn_pair.1.refs_1_
  11.7 10.4 %collective-permute-start.3 = (bf16[256,512]{1,0:T(8,128)(2,1)S(1)}, bf16[256,512]{1,0:T(8,128)(2,1)S(1)}, u32[]{:S(2)}, u32[]{:S(2)}) collective-permute-start(bf16[256,512]{1,0:T(8,128)(2,1)S(1)} %turn_pair.1.refs_1_), channel_id=1, source_target_pairs={{8,0},{28,4},{16,8},{4,12},{24,16},{12,20},{0,24},{20,28},{9,1},{2... | collective-permute-start | bytes 786440 | tf_op jit(solution)/shard_map/ppermute | solution.py:246
  22.1 2.0 %collective-permute-start.5 = (bf16[256,512]{1,0:T(8,128)(2,1)S(1)}, bf16[256,512]{1,0:T(8,128)(2,1)S(1)}, u32[]{:S(2)}, u32[]{:S(2)}) collective-permute-start(bf16[256,512]{1,0:T(8,128)(2,1)S(1)} %turn_pair.1.refs_1_), channel_id=1, source_target_pairs={{28,0},{8,4},{4,8},{16,12},{12,16},{24,20},{20,24},{0,28},{29,1},{... | collective-permute-start | bytes 786440 | tf_op jit(solution)/shard_map/ppermute | solution.py:247
  24.1 3.9 %collective-permute-done.3.refs_2_ = bf16[256,512]{1,0:T(8,128)(2,1)S(1)} collective-permute-done((bf16[256,512]{1,0:T(8,128)(2,1)S(1)}, bf16[256,512]{1,0:T(8,128)(2,1)S(1)}, u32[]{:S(2)}, u32[]{:S(2)}) %collective-permute-start.3) | collective-permute-done | bytes 262176 | tf_op jit(solution)/shard_map/ppermute | solution.py:246
  28.0 5.2 %collective-permute-start.4 = (bf16[256,512]{1,0:T(8,128)(2,1)S(1)}, bf16[256,512]{1,0:T(8,128)(2,1)S(1)}, u32[]{:S(2)}, u32[]{:S(2)}) collective-permute-start(bf16[256,512]{1,0:T(8,128)(2,1)S(1)} %collective-permute-done.3.refs_2_), channel_id=1, source_target_pairs={{28,0},{8,4},{4,8},{16,12},{12,16},{24,20},{20,24},{0,28},{29,1},{... | collective-permute-start | bytes 786440 | tf_op jit(solution)/shard_map/ppermute | solution.py:248
  33.2 0.2 select_convert_fusion.2
  33.4 0.0 collective-permute-done.1
  33.4 0.5 %turn.1.refs_0_ = bf16[4096,128]{1,0:T(8,128)(2,1)S(1)} custom-call(bf16[128,4096]{1,0:T(8,128)(2,1)S(1)} %bitcast.21, f32[256,128]{1,0:T(8,128)S(1)} %get-tuple-element.22.cosine_ref, f32[256,128]{1,0:T(8,128)S(1)} %get-tuple-element.21.sine_ref), custom_call_target="tpu_custom_call" | custom-call | tf_op jit(solution)/shard_map/turn/pallas_call | solution.py:93
  33.9 0.2 collective-permute-done.5.refs_3_
  34.1 3.8 %attend.2 = (f32[4096,256]{1,0:T(8,128)S(1)}, f32[4096,128]{1,0:T(8,128)S(1)}) custom-call(bf16[4096,128]{1,0:T(8,128)(2,1)S(1)} %turn.1.refs_0_, bf16[256,512]{1,0:T(8,128)(2,1)S(1)} %turn_pair.1.refs_1_, bf16[256,512]{1,0:T(8,128)(2,1)S(1)} %collective-permute-done.3.refs_2_, bf16[256,512]{1,0:T(8,128)(2,1)S(1)} %collective-permute-done.5.refs_3_, ...), custom_call_target="tpu_custom_call" | custom-call | flops 1000 | bytes 1000 | tf_op jit(solution)/shard_map/attend/pallas_call | solution.py:198
  38.0 1.4 %collective-permute-done.4.refs_1_ = bf16[256,512]{1,0:T(8,128)(2,1)S(1)} collective-permute-done((bf16[256,512]{1,0:T(8,128)(2,1)S(1)}, bf16[256,512]{1,0:T(8,128)(2,1)S(1)}, u32[]{:S(2)}, u32[]{:S(2)}) %collective-permute-start.4) | collective-permute-done | bytes 262176 | tf_op jit(solution)/shard_map/ppermute | solution.py:248
  39.3 2.6 %attend.3 = bf16[128,4096]{1,0:T(8,128)(2,1)} custom-call(bf16[4096,128]{1,0:T(8,128)(2,1)S(1)} %turn.1.refs_0_, bf16[256,512]{1,0:T(8,128)(2,1)S(1)} %collective-permute-done.4.refs_1_, bf16[256,128]{1,0:T(8,128)(2,1)S(1)} %get-tuple-element.29.refs_2_, f32[4096,256]{1,0:T(8,128)S(1)} %get-tuple-element.11.refs_3_, f32[4096,128]{1,0:T(8,128)S(1)} %get-tuple-element.12.refs_4_), custom_call_target="tpu_custom_call" | custom-call | flops 1000 | bytes 1000 | tf_op jit(solution)/shard_map/attend/pallas_call | solution.py:198
  (3 shorter events, 0.0 us)
Async XLA Ops:
  0.9 7.7 %collective-permute-start = (bf16[128,512]{1,0:T(8,128)(2,1)S(1)}, bf16[128,512]{1,0:T(8,128)(2,1)S(1)}, u32[]{:S(2)}, u32[]{:S(2)}) collective-permute-start(bf16[128,512]{1,0:T(8,128)(2,1)S(1)} %pad_maximum_fusion.1), channel_id=1, source_target_pairs={{480,0},{0,32},{32,64},{64,96},{96,128},{128,160},{160,192},{192,2... | collective-permute-start | bytes 393224 | tf_op jit(solution)/shard_map/ppermute | solution.py:22
  3.6 8.0 %collective-permute-start.2 = (bf16[128,512]{1,0:T(8,128)(2,1)S(1)}, bf16[128,512]{1,0:T(8,128)(2,1)S(1)}, u32[]{:S(2)}, u32[]{:S(2)}) collective-permute-start(bf16[128,512]{1,0:T(8,128)(2,1)S(1)} %pad_maximum_fusion.1), channel_id=1, source_target_pairs={{484,0},{480,4},{492,8},{488,12},{500,16},{496,20},{508,24},{504,2... | collective-permute-start | bytes 393224 | tf_op jit(solution)/shard_map/ppermute | solution.py:215
  8.6 24.8 %collective-permute-start.1 = (bf16[1,128,4096]{2,1,0:T(8,128)(2,1)}, bf16[1,128,4096]{2,1,0:T(8,128)(2,1)S(1)}, u32[]{:S(2)}, u32[]{:S(2)}) collective-permute-start(bf16[1,128,4096]{2,1,0:T(8,128)(2,1)} %param.7), channel_id=1, source_target_pairs={{480,0},{0,32},{32,64},{64,96},{96,128},{128,160},{160,192},{192,2... | collective-permute-start | bytes 3145736 | tf_op jit(solution)/shard_map/ppermute | solution.py:22
  11.7 16.3 %collective-permute-start.3 = (bf16[256,512]{1,0:T(8,128)(2,1)S(1)}, bf16[256,512]{1,0:T(8,128)(2,1)S(1)}, u32[]{:S(2)}, u32[]{:S(2)}) collective-permute-start(bf16[256,512]{1,0:T(8,128)(2,1)S(1)} %turn_pair.1.refs_1_), channel_id=1, source_target_pairs={{8,0},{28,4},{16,8},{4,12},{24,16},{12,20},{0,24},{20,28},{9,1},{2... | collective-permute-start | bytes 786440 | tf_op jit(solution)/shard_map/ppermute | solution.py:246
  22.1 12.1 %collective-permute-start.5 = (bf16[256,512]{1,0:T(8,128)(2,1)S(1)}, bf16[256,512]{1,0:T(8,128)(2,1)S(1)}, u32[]{:S(2)}, u32[]{:S(2)}) collective-permute-start(bf16[256,512]{1,0:T(8,128)(2,1)S(1)} %turn_pair.1.refs_1_), channel_id=1, source_target_pairs={{28,0},{8,4},{4,8},{16,12},{12,16},{24,20},{20,24},{0,28},{29,1},{... | collective-permute-start | bytes 786440 | tf_op jit(solution)/shard_map/ppermute | solution.py:247
  28.0 11.4 %collective-permute-start.4 = (bf16[256,512]{1,0:T(8,128)(2,1)S(1)}, bf16[256,512]{1,0:T(8,128)(2,1)S(1)}, u32[]{:S(2)}, u32[]{:S(2)}) collective-permute-start(bf16[256,512]{1,0:T(8,128)(2,1)S(1)} %collective-permute-done.3.refs_2_), channel_id=1, source_target_pairs={{28,0},{8,4},{4,8},{16,12},{12,16},{24,20},{20,24},{0,28},{29,1},{... | collective-permute-start | bytes 786440 | tf_op jit(solution)/shard_map/ppermute | solution.py:248

commit v6 on v5

--- a/solution.py
+++ b/solution.py
@@ -245,6 +245,7 @@
     pair_rows = turn_pair(own_rows, partner_rows, cosine, sine)
     second = lax.ppermute(pair_rows, "ctx", route(2))
     beside_rows = lax.ppermute(pair_rows, "ctx", route(-1))
+    second, masks = lax.optimization_barrier((second, masks))
     across = lax.ppermute(second, "ctx", route(-1))
     queries = turn_queries(query_in[0], cosine, sine)
     carried = ()

time: 42.2 us -> 42.2 us (level)
  no operation moved by 1% of the time
where the time goes in v6:
time: 42.2 us; the launch traced here: 41.9 us
  starting transfers between devices  24.6 us (58%)
  Pallas kernels  7.02 us (17%)
  waiting for transfers between devices  6.72 us (16%)
  other arithmetic  2.39 us (6%)
  local copies, waits for them, and re-layouts  0.98 us (2%)
    ppermute x1, starting transfers between devices, per_device(): second = lax.ppermute(pair_rows, 'ctx', route(2))  10.4 us
    pallas_call x2, Pallas kernels, attend(): pl.pallas_call(partial(attend_kernel, pieces=len(pieces), first=not carri...  6.4 us
    ppermute x1, starting transfers between devices, per_device(): across = lax.ppermute(second, 'ctx', route(-1))  5.18 us
    ppermute x1, starting transfers between devices, per_device(): lax.ppermute(rows, ('section', 'ctx'), [((s - 1) % sections * owners + (c...  3.73 us
    ppermute x1, waiting for transfers between devices, per_device(): second = lax.ppermute(pair_rows, 'ctx', route(2))  3.7 us
    ppermute x2, starting transfers between devices, shifted(): return lax.ppermute(block, axis, route)  3.36 us
    ppermute x1, starting transfers between devices, per_device(): beside_rows = lax.ppermute(pair_rows, 'ctx', route(-1))  1.98 us
    ppermute x1, waiting for transfers between devices, per_device(): across = lax.ppermute(second, 'ctx', route(-1))  1.27 us
  transfers between devices with their start and end apart: 6, of which 4 were waited for; matrix products, arithmetic and copies ran while one was open for 6% of the time, Pallas kernels for 11%

profile of v6, /device:TPU:1, one launch (start us, length us, event | category | flops | bytes accessed | tf_op | source)
XLA Modules:
  0.0 41.9 jit_solution(8425585611927883494)
XLA Ops:
  0.0 0.9 %pad_maximum_fusion.1 = bf16[128,512]{1,0:T(8,128)(2,1)S(1)} fusion(bf16[128,256]{1,0:T(8,128)(2,1)} %bitcast.22, bf16[128,256]{1,0:T(8,128)(2,1)} %bitcast.23), kind=kLoop, calls=%fused_computation.1 | loop fusion | flops 262144 | bytes 262144 | tf_op jit(solution)/shard_map/concatenate | solution.py:213
  0.9 2.7 %collective-permute-start = (bf16[128,512]{1,0:T(8,128)(2,1)S(1)}, bf16[128,512]{1,0:T(8,128)(2,1)S(1)}, u32[]{:S(2)}, u32[]{:S(2)}) collective-permute-start(bf16[128,512]{1,0:T(8,128)(2,1)S(1)} %pad_maximum_fusion.1), channel_id=1, source_target_pairs={{480,0},{0,32},{32,64},{64,96},{96,128},{128,160},{160,192},{192,2... | collective-permute-start | bytes 393224 | tf_op jit(solution)/shard_map/ppermute | solution.py:22
  3.6 3.7 %collective-permute-start.2 = (bf16[128,512]{1,0:T(8,128)(2,1)S(1)}, bf16[128,512]{1,0:T(8,128)(2,1)S(1)}, u32[]{:S(2)}, u32[]{:S(2)}) collective-permute-start(bf16[128,512]{1,0:T(8,128)(2,1)S(1)} %pad_maximum_fusion.1), channel_id=1, source_target_pairs={{484,0},{480,4},{492,8},{488,12},{500,16},{496,20},{508,24},{504,2... | collective-permute-start | bytes 393224 | tf_op jit(solution)/shard_map/ppermute | solution.py:215
  7.4 1.2 %collective-permute-done.own_ref = bf16[128,512]{1,0:T(8,128)(2,1)S(1)} collective-permute-done((bf16[128,512]{1,0:T(8,128)(2,1)S(1)}, bf16[128,512]{1,0:T(8,128)(2,1)S(1)}, u32[]{:S(2)}, u32[]{:S(2)}) %collective-permute-start) | collective-permute-done | bytes 131104 | tf_op jit(solution)/shard_map/ppermute | solution.py:22
  8.6 0.7 %collective-permute-start.1 = (bf16[1,128,4096]{2,1,0:T(8,128)(2,1)}, bf16[1,128,4096]{2,1,0:T(8,128)(2,1)S(1)}, u32[]{:S(2)}, u32[]{:S(2)}) collective-permute-start(bf16[1,128,4096]{2,1,0:T(8,128)(2,1)} %param.7), channel_id=1, source_target_pairs={{480,0},{0,32},{32,64},{64,96},{96,128},{128,160},{160,192},{192,2... | collective-permute-start | bytes 3145736 | tf_op jit(solution)/shard_map/ppermute | solution.py:22
  9.3 1.0 %fusion.9 = (s32[128]{0:T(128)S(1)}, s32[128]{0:T(128)S(1)}, s32[128]{0:T(128)S(1)}, s32[128]{0:T(128)S(1)}, s32[128]{0:T(128)S(1)}, /*index=5*/s32[128]{0:T(128)S(1)}, s32[128]{0:T(128)S(1)}, s32[128]{0:T(128)S(1)}) fusion(s32[8,128]{1,0:T(8,128)} %bitcast.24, s32[]{:T(128)S(6)} %select_n.100, s32[]{:T(128)S(6)} %select_n.101, s32[]{:T(128)S(6)} %select_n.97, ...), kind=kLoop, calls=%fused_computation.34 | loop fusion | bytes 8224 | tf_op jit(solution)/shard_map/jit(dynamic_index_in_dim)/squeeze | solution.py:228
  10.3 1.3 %sine_multiply_fusion = (f32[256,128]{1,0:T(8,128)S(1)}, f32[256,128]{1,0:T(8,128)S(1)}) fusion(f32[128]{0:T(128)} %constant.105.clone, f32[128]{0:T(128)} %constant.103.clone, f32[256]{0:T(256)S(1)} %get-tuple-element.35, f32[128]{0:T(128)} %constant.104.clone, f32[256]{0:T(256)S(1)} %get-tuple-element.34), kind=kLoop, calls=%fused_computation.6 | loop fusion | flops 131072 | bytes 265728 | tf_op jit(solution)/shard_map/mul | solution.py:44
  11.6 0.0 collective-permute-done.2.partner_ref
  11.6 0.1 turn_pair.1.refs_1_
  11.7 10.4 %collective-permute-start.3 = (bf16[256,512]{1,0:T(8,128)(2,1)S(1)}, bf16[256,512]{1,0:T(8,128)(2,1)S(1)}, u32[]{:S(2)}, u32[]{:S(2)}) collective-permute-start(bf16[256,512]{1,0:T(8,128)(2,1)S(1)} %turn_pair.1.refs_1_), channel_id=1, source_target_pairs={{8,0},{28,4},{16,8},{4,12},{24,16},{12,20},{0,24},{20,28},{9,1},{2... | collective-permute-start | bytes 786440 | tf_op jit(solution)/shard_map/ppermute | solution.py:246
  22.1 0.2 select_convert_fusion
  22.3 2.0 %collective-permute-start.5 = (bf16[256,512]{1,0:T(8,128)(2,1)S(1)}, bf16[256,512]{1,0:T(8,128)(2,1)S(1)}, u32[]{:S(2)}, u32[]{:S(2)}) collective-permute-start(bf16[256,512]{1,0:T(8,128)(2,1)S(1)} %turn_pair.1.refs_1_), channel_id=1, source_target_pairs={{28,0},{8,4},{4,8},{16,12},{12,16},{24,20},{20,24},{0,28},{29,1},{... | collective-permute-start | bytes 786440 | tf_op jit(solution)/shard_map/ppermute | solution.py:247
  24.3 3.7 %collective-permute-done.3.refs_2_ = bf16[256,512]{1,0:T(8,128)(2,1)S(1)} collective-permute-done((bf16[256,512]{1,0:T(8,128)(2,1)S(1)}, bf16[256,512]{1,0:T(8,128)(2,1)S(1)}, u32[]{:S(2)}, u32[]{:S(2)}) %collective-permute-start.3) | collective-permute-done | bytes 262176 | tf_op jit(solution)/shard_map/ppermute | solution.py:246
  28.0 5.2 %collective-permute-start.4 = (bf16[256,512]{1,0:T(8,128)(2,1)S(1)}, bf16[256,512]{1,0:T(8,128)(2,1)S(1)}, u32[]{:S(2)}, u32[]{:S(2)}) collective-permute-start(bf16[256,512]{1,0:T(8,128)(2,1)S(1)} %collective-permute-done.3.refs_2_), channel_id=1, source_target_pairs={{28,0},{8,4},{4,8},{16,12},{12,16},{24,20},{20,24},{0,28},{29,1},{... | collective-permute-start | bytes 786440 | tf_op jit(solution)/shard_map/ppermute | solution.py:249
  33.2 0.0 collective-permute-done.1
  33.2 0.5 %turn.1.refs_0_ = bf16[4096,128]{1,0:T(8,128)(2,1)S(1)} custom-call(bf16[128,4096]{1,0:T(8,128)(2,1)S(1)} %bitcast.21, f32[256,128]{1,0:T(8,128)S(1)} %get-tuple-element.32.cosine_ref, f32[256,128]{1,0:T(8,128)S(1)} %get-tuple-element.31.sine_ref), custom_call_target="tpu_custom_call" | custom-call | tf_op jit(solution)/shard_map/turn/pallas_call | solution.py:93
  33.7 0.6 %collective-permute-done.5.refs_3_ = bf16[256,512]{1,0:T(8,128)(2,1)S(1)} collective-permute-done((bf16[256,512]{1,0:T(8,128)(2,1)S(1)}, bf16[256,512]{1,0:T(8,128)(2,1)S(1)}, u32[]{:S(2)}, u32[]{:S(2)}) %collective-permute-start.5) | collective-permute-done | bytes 262176 | tf_op jit(solution)/shard_map/ppermute | solution.py:247
  34.2 3.8 %attend.2 = (f32[4096,256]{1,0:T(8,128)S(1)}, f32[4096,128]{1,0:T(8,128)S(1)}) custom-call(bf16[4096,128]{1,0:T(8,128)(2,1)S(1)} %turn.1.refs_0_, bf16[256,512]{1,0:T(8,128)(2,1)S(1)} %turn_pair.1.refs_1_, bf16[256,512]{1,0:T(8,128)(2,1)S(1)} %collective-permute-done.3.refs_2_, bf16[256,512]{1,0:T(8,128)(2,1)S(1)} %collective-permute-done.5.refs_3_, ...), custom_call_target="tpu_custom_call" | custom-call | flops 1000 | bytes 1000 | tf_op jit(solution)/shard_map/attend/pallas_call | solution.py:198
  38.1 1.3 %collective-permute-done.4.refs_1_ = bf16[256,512]{1,0:T(8,128)(2,1)S(1)} collective-permute-done((bf16[256,512]{1,0:T(8,128)(2,1)S(1)}, bf16[256,512]{1,0:T(8,128)(2,1)S(1)}, u32[]{:S(2)}, u32[]{:S(2)}) %collective-permute-start.4) | collective-permute-done | bytes 262176 | tf_op jit(solution)/shard_map/ppermute | solution.py:249
  39.3 2.6 %attend.3 = bf16[128,4096]{1,0:T(8,128)(2,1)} custom-call(bf16[4096,128]{1,0:T(8,128)(2,1)S(1)} %turn.1.refs_0_, bf16[256,512]{1,0:T(8,128)(2,1)S(1)} %collective-permute-done.4.refs_1_, bf16[256,128]{1,0:T(8,128)(2,1)S(1)} %get-tuple-element.17.refs_2_, f32[4096,256]{1,0:T(8,128)S(1)} %get-tuple-element.21.refs_3_, f32[4096,128]{1,0:T(8,128)S(1)} %get-tuple-element.22.refs_4_), custom_call_target="tpu_custom_call" | custom-call | flops 1000 | bytes 1000 | tf_op jit(solution)/shard_map/attend/pallas_call | solution.py:198
  (3 shorter events, 0.0 us)
Async XLA Ops:
  0.9 7.7 %collective-permute-start = (bf16[128,512]{1,0:T(8,128)(2,1)S(1)}, bf16[128,512]{1,0:T(8,128)(2,1)S(1)}, u32[]{:S(2)}, u32[]{:S(2)}) collective-permute-start(bf16[128,512]{1,0:T(8,128)(2,1)S(1)} %pad_maximum_fusion.1), channel_id=1, source_target_pairs={{480,0},{0,32},{32,64},{64,96},{96,128},{128,160},{160,192},{192,2... | collective-permute-start | bytes 393224 | tf_op jit(solution)/shard_map/ppermute | solution.py:22
  3.6 8.0 %collective-permute-start.2 = (bf16[128,512]{1,0:T(8,128)(2,1)S(1)}, bf16[128,512]{1,0:T(8,128)(2,1)S(1)}, u32[]{:S(2)}, u32[]{:S(2)}) collective-permute-start(bf16[128,512]{1,0:T(8,128)(2,1)S(1)} %pad_maximum_fusion.1), channel_id=1, source_target_pairs={{484,0},{480,4},{492,8},{488,12},{500,16},{496,20},{508,24},{504,2... | collective-permute-start | bytes 393224 | tf_op jit(solution)/shard_map/ppermute | solution.py:215
  8.6 24.6 %collective-permute-start.1 = (bf16[1,128,4096]{2,1,0:T(8,128)(2,1)}, bf16[1,128,4096]{2,1,0:T(8,128)(2,1)S(1)}, u32[]{:S(2)}, u32[]{:S(2)}) collective-permute-start(bf16[1,128,4096]{2,1,0:T(8,128)(2,1)} %param.7), channel_id=1, source_target_pairs={{480,0},{0,32},{32,64},{64,96},{96,128},{128,160},{160,192},{192,2... | collective-permute-start | bytes 3145736 | tf_op jit(solution)/shard_map/ppermute | solution.py:22
  11.7 16.3 %collective-permute-start.3 = (bf16[256,512]{1,0:T(8,128)(2,1)S(1)}, bf16[256,512]{1,0:T(8,128)(2,1)S(1)}, u32[]{:S(2)}, u32[]{:S(2)}) collective-permute-start(bf16[256,512]{1,0:T(8,128)(2,1)S(1)} %turn_pair.1.refs_1_), channel_id=1, source_target_pairs={{8,0},{28,4},{16,8},{4,12},{24,16},{12,20},{0,24},{20,28},{9,1},{2... | collective-permute-start | bytes 786440 | tf_op jit(solution)/shard_map/ppermute | solution.py:246
  22.3 12.0 %collective-permute-start.5 = (bf16[256,512]{1,0:T(8,128)(2,1)S(1)}, bf16[256,512]{1,0:T(8,128)(2,1)S(1)}, u32[]{:S(2)}, u32[]{:S(2)}) collective-permute-start(bf16[256,512]{1,0:T(8,128)(2,1)S(1)} %turn_pair.1.refs_1_), channel_id=1, source_target_pairs={{28,0},{8,4},{4,8},{16,12},{12,16},{24,20},{20,24},{0,28},{29,1},{... | collective-permute-start | bytes 786440 | tf_op jit(solution)/shard_map/ppermute | solution.py:247
  28.0 11.4 %collective-permute-start.4 = (bf16[256,512]{1,0:T(8,128)(2,1)S(1)}, bf16[256,512]{1,0:T(8,128)(2,1)S(1)}, u32[]{:S(2)}, u32[]{:S(2)}) collective-permute-start(bf16[256,512]{1,0:T(8,128)(2,1)S(1)} %collective-permute-done.3.refs_2_), channel_id=1, source_target_pairs={{28,0},{8,4},{4,8},{16,12},{12,16},{24,20},{20,24},{0,28},{29,1},{... | collective-permute-start | bytes 786440 | tf_op jit(solution)/shard_map/ppermute | solution.py:249
